TPU v7x, 256 devices: a whole 4x4x8 slice. The times are simulated.
256 devices in a mesh: dp: 2 (over core), seq: 32 (over y, z), tensor: 4 (over x).
Axes of the slice: x: 4, y: 4, z: 8, core: 2. Of those that a mesh axis runs over, the one named last changes fastest.
Arguments:
- q_raw: bfloat16 [2, 8192, 3072], P('dp', 'seq', 'tensor'), may hold values from -240 to 240
- k_raw: bfloat16 [2, 8192, 3072], P('dp', 'seq', 'tensor'), may hold values from -240 to 240
- v_raw: bfloat16 [2, 8192, 3072], P('dp', 'seq', 'tensor'), may hold values from -6 to 6
- out_grad: bfloat16 [2, 8192, 3072], P('dp', 'seq', 'tensor'), may hold values from -54 to 54
- gain_q: float32 [128], replicated, may hold values from 0.5 to 6
- gain_k: float32 [128], replicated, may hold values from 0.5 to 6
- keep_list: int32 [2, 4096], P('dp'), may hold values from 0 to 8191, as said below
Outputs:
- q_grad: bfloat16 [2, 8192, 3072], P('dp', 'seq', 'tensor')
- k_grad: bfloat16 [2, 8192, 3072], P('dp', 'seq', 'tensor')
- v_grad: bfloat16 [2, 8192, 3072], P('dp', 'seq', 'tensor')
- gain_q_grad: float32 [128], replicated
- gain_k_grad: float32 [128], replicated
Inputs may be any that keep to these rules, and one draw needn't show every extreme that they name: `keep_list`: for each clip the list names 4096 different tokens of that clip. For every i and j, positions j * 128 to (j + 1) * 128 - 1 hold at most 8 of the tokens i * 256 to (i + 1) * 256 - 1, and for every j some i gives exactly 8.
All inputs are finite; a program needn't handle non-finite values.
Results may differ from a plain program's by a relative error of at most 0.008.
The roundings to bfloat16 on the way count: a program that leaves them out, or rounds other values in their place, can miss the bound.
Values may be sent and summed in bfloat16 or wider, within the bound.
A program may use at most 128 MiB of HBM per device.

v0:
```python
import math

import jax
import jax.numpy as jnp
from jax import lax
from jax.sharding import PartitionSpec as P

HD = 128


EPSILON = 1e-06


def key_span(row_total):
    return math.gcd(512, row_total)


def normalize(kept_rows, gain_vec, head_count):
    raw_rows = kept_rows.astype(jnp.float32).reshape(kept_rows.shape[0], head_count, -1)
    inverse = lax.rsqrt(jnp.mean(raw_rows * raw_rows, axis=-1) + EPSILON)
    normed = (raw_rows * inverse[..., None] * gain_vec).astype(jnp.bfloat16)
    return (raw_rows, inverse, normed)


def norm_grads(raw_rows, inverse, gain_vec, upstream):
    scaled = upstream * gain_vec
    inner = jnp.mean(scaled * raw_rows, axis=-1)
    row_grads = (
        inverse[..., None] * scaled - raw_rows * (inverse * inverse * inverse * inner)[..., None]
    )
    gain_term = jnp.sum(upstream * raw_rows * inverse[..., None], axis=(0, 1))
    return (row_grads, gain_term)


def online_stats(queries, grad_rows, key_blocks, value_blocks, scaling):
    row_count = queries.shape[0]
    head_count = queries.shape[1]

    def online_absorb(running, block_pair):
        highest, totals, weighted = running
        scores = (
            jnp.einsum("qhd,khd->hqk", queries, block_pair[0], preferred_element_type=jnp.float32)
            * scaling
        )
        grad_dots = jnp.einsum(
            "qhd,khd->hqk", grad_rows, block_pair[1], preferred_element_type=jnp.float32
        )
        new_top = jnp.maximum(highest, jnp.max(scores, axis=-1))
        shrink = jnp.exp(highest - new_top)
        exp_terms = jnp.exp(scores - new_top[..., None])
        return (
            (
                new_top,
                totals * shrink + jnp.sum(exp_terms, axis=-1),
                weighted * shrink + jnp.sum(exp_terms * grad_dots, axis=-1),
            ),
            None,
        )

    start_state = (
        jnp.full((head_count, row_count), -jnp.inf, jnp.float32),
        jnp.zeros((head_count, row_count), jnp.float32),
        jnp.zeros((head_count, row_count), jnp.float32),
    )
    final_state, _ = lax.scan(online_absorb, start_state, (key_blocks, value_blocks))
    return final_state


def score_grads(queries, grad_rows, key_rows, value_rows, log_norm, delta_rows, scaling):
    scores = (
        jnp.einsum("qhd,khd->hqk", queries, key_rows, preferred_element_type=jnp.float32) * scaling
    )
    weights = jnp.exp(scores - log_norm[..., None])
    grad_dots = jnp.einsum(
        "qhd,khd->hqk", grad_rows, value_rows, preferred_element_type=jnp.float32
    )
    dscore = (weights * (grad_dots - delta_rows[..., None])).astype(jnp.bfloat16)
    return (weights.astype(jnp.bfloat16), dscore)


def key_side(queries, key_rows, value_rows, grad_rows, scaling):
    row_count, head_part = (queries.shape[0], queries.shape[1])
    flat_width = head_part * HD
    all_keys, all_values = (
        lax.all_gather(key_rows.reshape(row_count, flat_width), "seq", axis=0, tiled=True),
        lax.all_gather(value_rows.reshape(row_count, flat_width), "seq", axis=0, tiled=True),
    )
    row_total = all_keys.shape[0]
    block_len = key_span(row_total)
    block_count = row_total // block_len
    key_blocks = all_keys.reshape(block_count, block_len, head_part, HD)
    value_blocks = all_values.reshape(block_count, block_len, head_part, HD)
    highest, totals, weighted = online_stats(queries, grad_rows, key_blocks, value_blocks, scaling)
    log_norm = highest + jnp.log(totals)
    delta_rows = weighted / totals

    def add_block(running, block_pair):
        weights, dscore = score_grads(
            queries, grad_rows, block_pair[0], block_pair[1], log_norm, delta_rows, scaling
        )
        return (
            running
            + jnp.einsum("hqk,khd->qhd", dscore, block_pair[0], preferred_element_type=jnp.float32),
            None,
        )

    zero_grad = jnp.zeros((row_count, head_part, HD), jnp.float32)
    query_grad, _ = lax.scan(add_block, zero_grad, (key_blocks, value_blocks))
    norm_all, delta_all = (
        lax.all_gather(log_norm, "seq", axis=1, tiled=True),
        lax.all_gather(delta_rows, "seq", axis=1, tiled=True),
    )
    pieces = (
        lax.all_gather(queries.reshape(row_count, flat_width), "seq", axis=0, tiled=True),
        lax.all_gather(grad_rows.reshape(row_count, flat_width), "seq", axis=0, tiled=True),
    )
    piece_rows = pieces[0].shape[0]
    sub_rows = key_span(piece_rows)
    sub_count = piece_rows // sub_rows
    norm_piece = norm_all.reshape(head_part, sub_count, sub_rows)
    delta_piece = delta_all.reshape(head_part, sub_count, sub_rows)

    def add_absorb(inner_run, inputs):
        query_block, grad_block, norm_block, delta_block = inputs
        weights, dscore = score_grads(
            query_block, grad_block, key_rows, value_rows, norm_block, delta_block, scaling
        )
        key_grad = inner_run[0] + jnp.einsum(
            "hqk,qhd->khd", dscore, query_block, preferred_element_type=jnp.float32
        )
        value_grad = inner_run[1] + jnp.einsum(
            "hqk,qhd->khd", weights, grad_block, preferred_element_type=jnp.float32
        )
        return ((key_grad, value_grad), None)

    inputs = (
        pieces[0].reshape(sub_count, sub_rows, head_part, HD),
        pieces[1].reshape(sub_count, sub_rows, head_part, HD),
        jnp.moveaxis(norm_piece, 1, 0),
        jnp.moveaxis(delta_piece, 1, 0),
    )
    result, _ = lax.scan(add_absorb, (zero_grad, zero_grad), inputs)
    key_grad, value_grad = result
    return (query_grad * scaling, key_grad * scaling, value_grad)


def on_device(q_raw, k_raw, v_raw, out_grad, gain_q, gain_k, keep_list):
    seq_count = lax.axis_size("seq")
    place = lax.axis_index("seq")
    span_len = q_raw.shape[1]
    width = q_raw.shape[2]
    head_count = width // HD
    share = span_len // 2
    slot_count = 2 * share // seq_count
    scaling = 1.0 / math.sqrt(HD)
    listing = keep_list[0].reshape(seq_count, share)
    source = listing // span_len
    owners = jnp.arange(seq_count, dtype=jnp.int32)
    onehot = (source[:, :, None] == owners[None, None, :]).astype(jnp.int32)
    slot_rank = jnp.sum((jnp.cumsum(onehot, axis=1) - 1) * onehot, axis=-1)
    target = jnp.where(
        source == place, owners[:, None] * slot_count + slot_rank, seq_count * slot_count
    ).reshape(-1)
    local_row = (listing - place * span_len).reshape(-1)
    table = jnp.zeros((seq_count * slot_count,), jnp.int32).at[target].set(local_row, mode="drop")
    filled = jnp.zeros((seq_count * slot_count,), jnp.int32).at[target].set(1, mode="drop")
    send_q = q_raw[0][table].reshape(seq_count, slot_count, width)
    send_k = k_raw[0][table].reshape(seq_count, slot_count, width)
    send_v = v_raw[0][table].reshape(seq_count, slot_count, width)
    send_g = out_grad[0][table].reshape(seq_count, slot_count, width)
    recv_q, recv_k, recv_v, recv_g = (
        lax.all_to_all(send_q, "seq", split_axis=0, concat_axis=0, tiled=True),
        lax.all_to_all(send_k, "seq", split_axis=0, concat_axis=0, tiled=True),
        lax.all_to_all(send_v, "seq", split_axis=0, concat_axis=0, tiled=True),
        lax.all_to_all(send_g, "seq", split_axis=0, concat_axis=0, tiled=True),
    )
    my_source = lax.dynamic_index_in_dim(source, place, 0, keepdims=False)
    my_rank = lax.dynamic_index_in_dim(slot_rank, place, 0, keepdims=False)
    flat_slot = my_source * slot_count + my_rank
    rows_q = recv_q.reshape(-1, width)[flat_slot]
    rows_k = recv_k.reshape(-1, width)[flat_slot]
    rows_v = recv_v.reshape(-1, width)[flat_slot].reshape(share, head_count, HD)
    rows_g = recv_g.reshape(-1, width)[flat_slot].reshape(share, head_count, HD)
    raw_q, inv_q, norm_q = normalize(rows_q, gain_q, head_count)
    raw_k, inv_k, norm_k = normalize(rows_k, gain_k, head_count)
    group_count = 2
    head_part = head_count // group_count
    grads_q, grads_k, grads_v = ([], [], [])
    for group_index in range(group_count):
        columns = slice(group_index * head_part, (group_index + 1) * head_part)
        part_q, part_k, part_v = key_side(
            norm_q[:, columns], norm_k[:, columns], rows_v[:, columns], rows_g[:, columns], scaling
        )
        grads_q.append(part_q)
        grads_k.append(part_k)
        grads_v.append(part_v)
    row_grads_q, term_q = norm_grads(raw_q, inv_q, gain_q, jnp.concatenate(grads_q, axis=1))
    row_grads_k, term_k = norm_grads(raw_k, inv_k, gain_k, jnp.concatenate(grads_k, axis=1))
    value_rows = jnp.concatenate(grads_v, axis=1)
    empty = jnp.zeros((seq_count * slot_count, width), jnp.bfloat16)
    back_q = (
        empty.at[flat_slot]
        .set(row_grads_q.reshape(share, width).astype(jnp.bfloat16))
        .reshape(seq_count, slot_count, width)
    )
    back_k = (
        empty.at[flat_slot]
        .set(row_grads_k.reshape(share, width).astype(jnp.bfloat16))
        .reshape(seq_count, slot_count, width)
    )
    back_v = (
        empty.at[flat_slot]
        .set(value_rows.reshape(share, width).astype(jnp.bfloat16))
        .reshape(seq_count, slot_count, width)
    )
    home_q, home_k, home_v = (
        lax.all_to_all(back_q, "seq", split_axis=0, concat_axis=0, tiled=True),
        lax.all_to_all(back_k, "seq", split_axis=0, concat_axis=0, tiled=True),
        lax.all_to_all(back_v, "seq", split_axis=0, concat_axis=0, tiled=True),
    )
    dest_row = jnp.where(filled > 0, table, span_len)
    blank = jnp.zeros((span_len, width), jnp.bfloat16)
    q_grad = blank.at[dest_row].set(home_q.reshape(-1, width), mode="drop")[None]
    k_grad = blank.at[dest_row].set(home_k.reshape(-1, width), mode="drop")[None]
    v_grad = blank.at[dest_row].set(home_v.reshape(-1, width), mode="drop")[None]
    gain_q_grad, gain_k_grad = lax.psum((term_q, term_k), ("dp", "seq", "tensor"))
    return (q_grad, k_grad, v_grad, gain_q_grad, gain_k_grad)


def solution(mesh):
    in_specs = (
        P("dp", "seq", "tensor"),
        P("dp", "seq", "tensor"),
        P("dp", "seq", "tensor"),
        P("dp", "seq", "tensor"),
        P(),
        P(),
        P("dp", None),
    )
    out_specs = (
        P("dp", "seq", "tensor"),
        P("dp", "seq", "tensor"),
        P("dp", "seq", "tensor"),
        P(),
        P(),
    )
    return jax.shard_map(
        on_device, mesh=mesh, in_specs=in_specs, out_specs=out_specs, check_vma=False
    )
```

profile of v0, /device:TPU:1, one launch (start us, length us, event | category | flops | bytes accessed | tf_op | source)
XLA Modules:
  0.0 903.3 jit_solution(11924867384054430078)
XLA Ops:
  13.1 15.5 %scatter_custom_fusion.1 = s32[256]{0:T(256)S(1)} fusion(s32[4096]{0:T(1024)S(1)} %bitcast.375, s32[4096]{0:T(1024)S(1)} %bitcast.377, s32[]{:T(128)} %constant.118.clone.1), kind=kCustom, calls=%fused_computation.218 | custom fusion | bytes 1028 | tf_op jit(solution)/shard_map/scatter | solution.py:165
  28.7 15.5 %scatter_custom_fusion = s32[256]{0:T(256)S(1)} fusion(s32[4096]{0:T(1024)S(1)} %bitcast.376, s32[4096]{0:T(1024)S(1)} %broadcast.295, s32[]{:T(128)} %constant.118.clone.1), kind=kCustom, calls=%fused_computation.220 | custom fusion | bytes 1028 | tf_op jit(solution)/shard_map/scatter | solution.py:166
  46.7 12.2 %all-to-all-start.1 = ((bf16[32,8,768]{2,1,0:T(8,128)(2,1)}), bf16[32,8,768]{2,1,0:T(8,128)(2,1)S(1)}, u32[]{:S(2)}, u32[]{:S(2)}) async-start(bf16[32,8,768]{2,1,0:T(8,128)(2,1)} %bitcast.12), calls=%async_computation.1 | async-start | bytes 786432 | tf_op jit(solution)/shard_map/all_to_all | solution.py:173
  59.1 11.4 %all-to-all-done.1 = bf16[32,8,768]{2,1,0:T(8,128)(2,1)S(1)} async-done(((bf16[32,8,768]{2,1,0:T(8,128)(2,1)}), bf16[32,8,768]{2,1,0:T(8,128)(2,1)S(1)}, u32[]{:S(2)}, u32[]{:S(2)}) %all-to-all-start.1) | async-done | bytes 393248 | tf_op jit(solution)/shard_map/all_to_all | solution.py:173
  73.7 18.0 %all_to_all.35 = bf16[32,8,768]{2,1,0:T(8,128)(2,1)S(1)} all-to-all(bf16[32,8,768]{2,1,0:T(8,128)(2,1)S(1)} %bitcast.353), channel_id=1, replica_groups=mesh['dp'=2,'seq'=32,'tensor'=4] {'seq'}, dimensions={0} | all-to-all | bytes 786432 | tf_op jit(solution)/shard_map/all_to_all | solution.py:174
  96.0 19.0 %all_to_all.36 = bf16[32,8,768]{2,1,0:T(8,128)(2,1)S(1)} all-to-all(bf16[32,8,768]{2,1,0:T(8,128)(2,1)S(1)} %bitcast.354), channel_id=1, replica_groups=mesh['dp'=2,'seq'=32,'tensor'=4] {'seq'}, dimensions={0} | all-to-all | bytes 786432 | tf_op jit(solution)/shard_map/all_to_all | solution.py:172
  118.3 20.4 %all_to_all.37 = bf16[32,8,768]{2,1,0:T(8,128)(2,1)S(1)} all-to-all(bf16[32,8,768]{2,1,0:T(8,128)(2,1)S(1)} %bitcast.352), channel_id=1, replica_groups=mesh['dp'=2,'seq'=32,'tensor'=4] {'seq'}, dimensions={0} | all-to-all | bytes 786432 | tf_op jit(solution)/shard_map/all_to_all | solution.py:175
  148.9 8.7 all-gather.13.cloned.1.call-done
  164.3 72.7 %all-gather.15.cloned.1.call-done = bf16[4096,384]{0,1:T(8,128)(2,1)} async-done(((bf16[128,384]{0,1:T(8,128)(2,1)}), bf16[4096,384]{0,1:T(8,128)(2,1)}) %all-gather.15.cloned.1.call-update) | async-done | bytes 3145744 | tf_op jit(solution)/shard_map/all_gather | solution.py:86
  243.8 26.8 %while.80 = (s32[]{:T(128)}, f32[3,128]{1,0:T(4,128)S(1)}, f32[3,128]{1,0:T(4,128)}, f32[3,128]{1,0:T(4,128)}, bf16[8,512,3,128]{3,1,2,0:T(8,128)(2,1)}, /*index...) while((s32[]{:T(128)}, f32[3,128]{1,0:T(4,128)S(1)}, ...), condition=%wide.region_17.18_spmd.clone, body=%wide.region_13.17_spmd.clone.sunk | while | flops 102042240 | bytes 3394800 | solution.py:65
  271.3 40.9 %all_gather.45 = f32[3,4096]{1,0:T(4,128)} all-gather(f32[3,128]{1,0:T(4,128)S(1)} %get-tuple-element.1255), channel_id=1, replica_groups=mesh['dp'=2,'seq'=32,'tensor'=4] {'seq'}, dimensions={1}, use_global_device_ids=true | all-gather | bytes 50688 | tf_op jit(solution)/shard_map/all_gather | solution.py:110
  312.3 39.3 %all_gather.47 = f32[3,4096]{1,0:T(4,128)} all-gather(f32[3,128]{1,0:T(4,128)S(1)} %get-tuple-element.1258), channel_id=1, replica_groups=mesh['dp'=2,'seq'=32,'tensor'=4] {'seq'}, dimensions={1}, use_global_device_ids=true | all-gather | bytes 50688 | tf_op jit(solution)/shard_map/all_gather | solution.py:111
  351.6 23.4 %while.81 = (s32[]{:T(128)}, f32[128,3,128]{0,2,1:T(8,128)S(1)}, bf16[8,512,3,128]{3,1,2,0:T(8,128)(2,1)}, bf16[128,3,128]{2,0,1:T(8,128)(2,1)S(1)}, f32[3,128]{...) while((s32[]{:T(128)}, f32[128,3,128]{0,2,1:T(8,128)S(1)}, ...), condition=%wide.region_19.20_spmd.clone, body=%wide.region_18.19_spmd.clone.sunk | while | flops 152076288 | bytes 3347066 | solution.py:108
  382.4 17.2 %all-gather.11.cloned.1.call-done = bf16[4096,384]{0,1:T(8,128)(2,1)} async-done(((bf16[128,384]{0,1:T(8,128)(2,1)}), bf16[4096,384]{0,1:T(8,128)(2,1)}) %all-gather.11.cloned.1.call-update) | async-done | bytes 3145744 | tf_op jit(solution)/shard_map/all_gather | solution.py:86
  406.4 22.2 %while.78 = (s32[]{:T(128)}, f32[3,128]{1,0:T(4,128)S(1)}, f32[3,128]{1,0:T(4,128)S(1)}, f32[3,128]{1,0:T(4,128)S(1)}, bf16[8,512,3,128]{3,1,2,0:T(8,128)(2,1)},...) while((s32[]{:T(128)}, f32[3,128]{1,0:T(4,128)S(1)}, ...), condition=%wide.region_10.11_spmd.clone, body=%wide.region_6.10_spmd.clone.sunk | while | flops 102042240 | bytes 3370112 | solution.py:65
  428.6 41.3 %all_gather.41 = f32[3,4096]{1,0:T(4,128)} all-gather(f32[3,128]{1,0:T(4,128)S(1)} %get-tuple-element.1315), channel_id=1, replica_groups=mesh['dp'=2,'seq'=32,'tensor'=4] {'seq'}, dimensions={1}, use_global_device_ids=true | all-gather | bytes 50688 | tf_op jit(solution)/shard_map/all_gather | solution.py:110
  469.9 38.6 %all_gather.43 = f32[3,4096]{1,0:T(4,128)} all-gather(f32[3,128]{1,0:T(4,128)S(1)} %get-tuple-element.1318), channel_id=1, replica_groups=mesh['dp'=2,'seq'=32,'tensor'=4] {'seq'}, dimensions={1}, use_global_device_ids=true | all-gather | bytes 50688 | tf_op jit(solution)/shard_map/all_gather | solution.py:111
  508.5 23.5 %while.79 = (s32[]{:T(128)}, f32[128,3,128]{0,2,1:T(8,128)S(1)}, bf16[8,512,3,128]{3,1,2,0:T(8,128)(2,1)}, bf16[128,3,128]{2,0,1:T(8,128)(2,1)S(1)}, f32[3,128]{...) while((s32[]{:T(128)}, f32[128,3,128]{0,2,1:T(8,128)S(1)}, ...), condition=%wide.region_12.13_spmd.clone, body=%wide.region_11.12_spmd.clone.sunk | while | flops 152076288 | bytes 3347066 | solution.py:108
  547.2 17.2 %all-gather.23.cloned.1.call-done = bf16[4096,384]{0,1:T(8,128)(2,1)} async-done(((bf16[128,384]{0,1:T(8,128)(2,1)}), bf16[4096,384]{0,1:T(8,128)(2,1)}) %all-gather.23.cloned.1.call-update) | async-done | bytes 3145744 | tf_op jit(solution)/shard_map/all_gather | solution.py:115
  571.2 74.0 %all-gather.17.cloned.1.call-done = bf16[4096,384]{0,1:T(8,128)(2,1)} async-done(((bf16[128,384]{0,1:T(8,128)(2,1)}), bf16[4096,384]{0,1:T(8,128)(2,1)}) %all-gather.17.cloned.1.call-update) | async-done | bytes 3145744 | tf_op jit(solution)/shard_map/all_gather | solution.py:114
  651.9 41.5 %while.83 = (s32[]{:T(128)}, f32[128,3,128]{0,2,1:T(8,128)S(1)}, f32[128,3,128]{0,2,1:T(8,128)S(1)}, bf16[8,512,3,128]{3,1,2,0:T(8,128)(2,1)}, bf16[128,3,128]{2...) while((s32[]{:T(128)}, f32[128,3,128]{0,2,1:T(8,128)S(1)}, ...), condition=%wide.region_26.27_spmd.clone, body=%wide.region_25.26_spmd.clone.sunk | while | flops 202702848 | bytes 4953739 | solution.py:142
  693.5 32.9 %all-gather.19.cloned.1.call-done = bf16[4096,384]{0,1:T(8,128)(2,1)} async-done(((bf16[128,384]{0,1:T(8,128)(2,1)}), bf16[4096,384]{0,1:T(8,128)(2,1)}) %all-gather.19.cloned.1.call-update) | async-done | bytes 3145744 | tf_op jit(solution)/shard_map/all_gather | solution.py:115
  733.2 47.3 %while.82 = (s32[]{:T(128)}, f32[128,3,128]{0,2,1:T(8,128)S(1)}, f32[128,3,128]{0,2,1:T(8,128)}, bf16[8,512,3,128]{3,1,2,0:T(8,128)(2,1)}, bf16[128,3,128]{2,0,1...) while((s32[]{:T(128)}, f32[128,3,128]{0,2,1:T(8,128)S(1)}, ...), condition=%wide.region_24.25_spmd.clone, body=%wide.region_23.24_spmd.clone.sunk | while | flops 202702848 | bytes 6526659 | solution.py:142
  806.5 81.7 %all-reduce = (f32[128]{0:T(128)}, f32[128]{0:T(128)}) all-reduce(f32[128]{0:T(128)S(1)} %get-tuple-element.755, f32[128]{0:T(128)S(1)} %get-tuple-element.753), channel_id=1, replica_groups=mesh['dp'=2,'seq'=32,'tensor'=4] {'dp','seq','tensor'}, use_global_device_ids=true, to_apply=%region_33.34 | all-reduce | flops 256 | bytes 2048 | tf_op jit(solution)/shard_map/psum | solution.py:226
  (508 shorter events, 309.1 us)
Async XLA Ops:
  7.2 37.5 %copy-start = (bf16[1,256,768]{2,1,0:T(8,128)(2,1)S(1)}, bf16[1,256,768]{2,1,0:T(8,128)(2,1)}, u32[]{:S(2)}) copy-start(bf16[1,256,768]{2,1,0:T(8,128)(2,1)} %param.20) | copy-start | bytes 1179652
  46.7 23.8 %all-to-all-start.1 = ((bf16[32,8,768]{2,1,0:T(8,128)(2,1)}), bf16[32,8,768]{2,1,0:T(8,128)(2,1)S(1)}, u32[]{:S(2)}, u32[]{:S(2)}) async-start(bf16[32,8,768]{2,1,0:T(8,128)(2,1)} %bitcast.12), calls=%async_computation.1 | async-start | bytes 786432 | tf_op jit(solution)/shard_map/all_to_all | solution.py:173
  58.8 98.7 %all-gather.13.cloned.1.call-start = ((), (), s32[]{:S(2)}) async-start(), calls=%async_computation.9 | async-start | bytes 3244032 | tf_op jit(solution)/shard_map/all_gather | solution.py:85
  71.6 76.3 %copy-start.38 = (f32[128,6]{0,1:T(8,128)}, f32[128,6]{0,1:T(8,128)S(1)}, u32[]{:S(2)}) copy-start(f32[128,6]{0,1:T(8,128)S(1)} %add_rsqrt_fusion) | copy-start | bytes 9220
  72.4 164.6 %all-gather.15.cloned.1.call-start = ((), (), s32[]{:S(2)}) async-start(), calls=%async_computation.10 | async-start | bytes 3244032 | tf_op jit(solution)/shard_map/all_gather | solution.py:86
  93.4 281.6 %all-gather.9.cloned.1.call-start = ((), (), s32[]{:S(2)}) async-start(), calls=%async_computation.7 | async-start | bytes 3244032 | tf_op jit(solution)/shard_map/all_gather | solution.py:85
  94.2 305.5 %all-gather.11.cloned.1.call-start = ((), (), s32[]{:S(2)}) async-start(), calls=%async_computation.8 | async-start | bytes 3244032 | tf_op jit(solution)/shard_map/all_gather | solution.py:86
  94.8 445.7 %all-gather.21.cloned.1.call-start = ((), (), s32[]{:S(2)}) async-start(), calls=%async_computation.13 | async-start | bytes 3244032 | tf_op jit(solution)/shard_map/all_gather | solution.py:114
  116.2 30.7 %copy-start.40 = (f32[128,6]{0,1:T(8,128)}, f32[128,6]{0,1:T(8,128)S(1)}, u32[]{:S(2)}) copy-start(f32[128,6]{0,1:T(8,128)S(1)} %add_rsqrt_fusion.1) | copy-start | bytes 9220
  117.0 447.4 %all-gather.23.cloned.1.call-start = ((), (), s32[]{:S(2)}) async-start(), calls=%async_computation.14 | async-start | bytes 3244032 | tf_op jit(solution)/shard_map/all_gather | solution.py:115
  118.3 27.7 %copy-start.31 = (bf16[128,3,128]{0,2,1:T(8,128)(2,1)S(1)}, bf16[128,3,128]{0,2,1:T(8,128)(2,1)}, u32[]{:S(2)}) copy-start(bf16[128,3,128]{0,2,1:T(8,128)(2,1)} %get-tuple-element.875) | copy-start | bytes 294916
  140.4 504.7 %all-gather.17.cloned.1.call-start = ((), (), s32[]{:S(2)}) async-start(), calls=%async_computation.11 | async-start | bytes 3244032 | tf_op jit(solution)/shard_map/all_gather | solution.py:114
  141.1 585.3 %all-gather.19.cloned.1.call-start = ((), (), s32[]{:S(2)}) async-start(), calls=%async_computation.12 | async-start | bytes 3244032 | tf_op jit(solution)/shard_map/all_gather | solution.py:115
  243.8 107.7 %copy-start.8 = (f32[128,3,128]{0,2,1:T(8,128)S(1)}, f32[128,3,128]{0,2,1:T(8,128)}, u32[]{:S(2)}) copy-start(f32[128,3,128]{0,2,1:T(8,128)} %custom-call.7) | copy-start | bytes 589828
  406.4 102.1 %copy-start.7 = (f32[128,3,128]{0,2,1:T(8,128)S(1)}, f32[128,3,128]{0,2,1:T(8,128)}, u32[]{:S(2)}) copy-start(f32[128,3,128]{0,2,1:T(8,128)} %custom-call.3) | copy-start | bytes 589828
  535.1 248.9 %all-to-all-start.4 = ((bf16[32,8,768]{2,1,0:T(8,128)(2,1)}), bf16[32,8,768]{2,1,0:T(8,128)(2,1)}, u32[]{:S(2)}, u32[]{:S(2)}) async-start(bf16[32,8,768]{2,1,0:T(8,128)(2,1)} %bitcast.30), calls=%async_computation.4 | async-start | bytes 786432 | tf_op jit(solution)/shard_map/all_to_all | solution.py:217
  693.5 36.3 %copy-start.15 = (f32[128,3,128]{0,2,1:T(8,128)}, f32[128,3,128]{0,2,1:T(8,128)S(1)}, u32[]{:S(2)}) copy-start(f32[128,3,128]{0,2,1:T(8,128)S(1)} %get-tuple-element.284) | copy-start | bytes 589828
  733.2 47.4 %copy-start.18 = (f32[128,768]{0,1:T(8,128)S(1)}, f32[128,768]{0,1:T(8,128)}, u32[]{:S(2)}) copy-start(f32[128,768]{0,1:T(8,128)} %copy-done.17) | copy-start | bytes 1179652
  733.2 47.4 %copy-start.39 = (f32[128,6]{0,1:T(8,128)S(1)}, f32[128,6]{0,1:T(8,128)}, u32[]{:S(2)}) copy-start(f32[128,6]{0,1:T(8,128)} %copy-done.38) | copy-start | bytes 9220
  733.2 47.4 %copy-start.51 = (f32[128]{0:T(128)S(1)}, f32[128]{0:T(128)}, u32[]{:S(2)}) copy-start(f32[128]{0:T(128)} %param.24) | copy-start | bytes 1540
  733.2 47.6 %copy-start.43 = (f32[128,6]{0,1:T(8,128)S(1)}, f32[128,6]{0,1:T(8,128)}, u32[]{:S(2)}) copy-start(f32[128,6]{0,1:T(8,128)} %copy-done.42) | copy-start | bytes 9220
  781.7 114.3 %copy-start.1 = (bf16[1,256,768]{2,1,0:T(8,128)(2,1)S(1)}, bf16[1,256,768]{2,1,0:T(8,128)(2,1)}, u32[]{:S(2)}) copy-start(bf16[1,256,768]{2,1,0:T(8,128)(2,1)} %param.20) | copy-start | bytes 1179652
  784.1 16.9 %all-to-all-start.5 = ((bf16[32,8,768]{2,1,0:T(8,128)(2,1)}), bf16[32,8,768]{2,1,0:T(8,128)(2,1)S(1)}, u32[]{:S(2)}, u32[]{:S(2)}) async-start(bf16[32,8,768]{2,1,0:T(8,128)(2,1)} %bitcast.49), calls=%async_computation.5 | async-start | bytes 786432 | tf_op jit(solution)/shard_map/all_to_all | solution.py:218
  801.0 92.5 %all-to-all-start.6 = ((bf16[32,8,768]{2,1,0:T(8,128)(2,1)}), bf16[32,8,768]{2,1,0:T(8,128)(2,1)S(1)}, u32[]{:S(2)}, u32[]{:S(2)}) async-start(bf16[32,8,768]{2,1,0:T(8,128)(2,1)} %bitcast.53), calls=%async_computation.6 | async-start | bytes 786432 | tf_op jit(solution)/shard_map/all_to_all | solution.py:219
  (83 other events, 587.6 us)
Sparse Core Ops, SparseCore 0:
  72.5 84.9 all-gather.12
  160.0 76.9 all-gather.14
  239.5 79.0 all-gather.8
  320.9 78.7 all-gather.10
  402.0 78.9 all-gather.20
  483.3 81.0 all-gather.22
  566.9 78.2 all-gather.16
  647.6 78.7 all-gather.18
where the time goes:
time: 917 us; the launch traced here: 903 us
  blocking collectives  299 us (33%)
  waiting for transfers between devices  244 us (27%)
  matrix products  158 us (17%)
  local copies, waits for them, and re-layouts  140 us (15%)
  starting transfers between devices  29.8 us (3%)
  between operations  15.6 us (2%)
  other arithmetic  14.1 us (2%)
    all_gather x2, waiting for transfers between devices, key_side(): lax.all_gather(value_rows.reshape(row_count, flat_width), 'seq', axis=0,...  90 us
    all_gather x2, blocking collectives, key_side(): lax.all_gather(log_norm, 'seq', axis=1, tiled=True)  82.3 us
    psum x1, blocking collectives, on_device(): lax.psum((term_q, term_k), ('dp', 'seq', 'tensor'))  81.7 us
    all_gather x2, blocking collectives, key_side(): lax.all_gather(delta_rows, 'seq', axis=1, tiled=True)  77.9 us
    all_gather x2, waiting for transfers between devices, key_side(): lax.all_gather(queries.reshape(row_count, flat_width), 'seq', axis=0, til...  74 us
    unnamed x118, local copies, waits for them, and re-layouts  60.1 us
    all_gather x2, waiting for transfers between devices, key_side(): lax.all_gather(grad_rows.reshape(row_count, flat_width), 'seq', axis=0, t...  50.1 us
    dot_general x32, matrix products, score_grads(): jnp.einsum('qhd,khd->hqk', queries, key_rows, preferred_element_type=jnp....  41.7 us
  transfers between devices with their start and end apart: 12, of which 8 were waited for; matrix products, arithmetic and copies ran while one was open for 28% of the time, Pallas kernels for 0%

commit v1 on v0

v1 whole, which is shorter than its diff:
```python
import math

import jax
import jax.numpy as jnp
from jax import lax
from jax.experimental import pallas as pl
from jax.experimental.pallas import tpu as pltpu
from jax.sharding import PartitionSpec as P

MESH = pl.DeviceIdType.MESH
HD = 128
EPSILON = 1e-06
SEQ = 32
SPAN = 256
SHARE = 128
SLOTS = 8
HEAD_PART = 6
UNITS = 6
ROWS = UNITS * SHARE
CHUNK = UNITS * SLOTS
FLAT = SEQ * CHUNK
MEMBERS = 16
KEPT = SEQ * SHARE
TILE = 256
TILES = ROWS // TILE
SCALING = 1.0 / math.sqrt(HD)
LOG2E = 1.4426950408889634
VMEM_LIMIT = 56 * 1024 * 1024

NT = (((1,), (1,)), ((), ()))

PATHS = (
    (0, 0, 0, 768, 0, (1, 2), None, None),
    (0, 1, 0, 768, 0, (1,), 1, 2),
    (1, None, 0, 768, 0, (0, 2), None, None),
    (2, 0, 0, 768, 0, (1,), 1, 0),
    (2, 1, 0, 256, 0, (1,), 1, 0),
    (2, 1, 256, 512, 1, (3, 4, 5), None, None),
    (3, None, 0, 768, 1, (2, 4), 2, 5),
    (4, None, 0, 768, 1, (5, 3), 5, 2),
    (5, 0, 0, 512, 1, (2, 3, 4), None, None),
    (5, 0, 512, 256, 2, (6,), 6, 7),
    (5, 1, 0, 768, 2, (6,), 6, 7),
    (6, None, 0, 768, 2, (5, 7), None, None),
    (7, 0, 0, 768, 2, (6, 5), None, None),
    (7, 1, 0, 768, 2, (6,), 6, 5),
)


def place(group, member):
    chip, core = member // 2, member % 2
    dz, dy = chip // 2, ((chip + 1) // 2) % 2
    y = 2 * (group // 2) + dy
    z = 4 * (group % 2) + dz
    return core, y * 8 + z


def my_place(dp, s):
    y, z = s // 8, s % 8
    dy, dz = y % 2, z % 4
    chip = 2 * dz + (dy + dz) % 2
    group = 2 * (y // 2) + z // 4
    return group, chip


def among(value, options):
    hit = value == options[0]
    for option in options[1:]:
        hit = hit | (value == option)
    return hit


def one_hot(hit):
    return jnp.where(hit, 1.0, 0.0).astype(jnp.bfloat16)


def inverse_norm(x):
    return lax.rsqrt(jnp.mean(x * x, axis=-1, keepdims=True) + EPSILON)


def norm_grads(raw, gain, upstream):
    raw = raw.astype(jnp.float32)
    inverse = inverse_norm(raw)
    scaled = upstream * gain
    inner = jnp.mean(scaled * raw, axis=-1, keepdims=True)
    grads = inverse * scaled - raw * (inverse * inverse * inverse * inner)
    terms = upstream * raw * inverse
    return grads, jnp.sum(terms.reshape(-1, 8, HD), axis=0)


def lane_fold(x, fold):
    parts = [x[:, i * 128 : (i + 1) * 128] for i in range(x.shape[1] // 128)]
    total = parts[0]
    for part in parts[1:]:
        total = fold(total, part)
    return total


def core_kernel(
    slot_ref,
    row_ref,
    enc_ref,
    k_ref,
    v_ref,
    q_ref,
    g_ref,
    gain_q_ref,
    gain_k_ref,
    home_ref,
    back_ref,
    total_ref,
    slots,
    arrived,
    other,
    codes,
    pick,
    full,
    raw,
    scores_ref,
    dots_ref,
    q_grad,
    q_slots,
    kv_slots,
    stats,
    terms,
    parts,
    partial,
    cross,
    enc_sem,
    route_send,
    route_recv,
    pair_send,
    pair_recv,
    path_send,
    path_recv,
    pass_send,
    hand_send,
    hand_recv,
    stat_send,
    stat_recv,
    home_send,
    home_recv,
    part_sem,
    cross_send,
    cross_recv,
):
    dp, s, x = lax.axis_index("dp"), lax.axis_index("seq"), lax.axis_index("tensor")
    group, chip = my_place(dp, s)
    clip = group // 2
    me = 2 * chip + dp
    seat = (group % 2) * MEMBERS + me
    sibling = (1 - dp, s, x)
    corner = dp * 4 + x
    same = clip == dp

    def remote(src, dst, send_sem, recv_sem, device):
        return pltpu.make_async_remote_copy(
            src_ref=src, dst_ref=dst, send_sem=send_sem, recv_sem=recv_sem, device_id=device, device_id_type=MESH
        )


    barrier = pltpu.get_barrier_semaphore()

    def greet(i, _):
        @pl.when((i // SEQ != dp) | (i % SEQ != s))
        def _():
            pl.semaphore_signal(barrier, inc=1, device_id=(i // SEQ, i % SEQ, x), device_id_type=MESH)

        return 0

    lax.fori_loop(0, 2 * SEQ, greet, 0)

    def greet_corner(i, _):
        @pl.when(i % 4 != x)
        def _():
            pl.semaphore_signal(barrier, inc=1, device_id=(i // 4, s, i % 4), device_id_type=MESH)

        return 0

    lax.fori_loop(0, 8, greet_corner, 0)


    step = 512
    iota = lax.broadcasted_iota(jnp.int32, (SPAN, step), 0)
    take = jnp.zeros((SPAN, SPAN), jnp.float32)
    back = jnp.zeros((SPAN, SPAN), jnp.float32)
    for c in range(KEPT // step):
        cols = slice(c * step, (c + 1) * step)
        a = one_hot(iota == slot_ref[:, cols])
        b = one_hot(iota == row_ref[:, cols])
        take += lax.dot_general(a, b, NT, preferred_element_type=jnp.float32)
        back += lax.dot_general(b, a, NT, preferred_element_type=jnp.float32)
    take = take.astype(jnp.bfloat16)
    back_ref[...] = back.astype(jnp.bfloat16)

    def to_slots(i, ref):
        rows = jnp.dot(take, ref[...], preferred_element_type=jnp.float32).astype(jnp.bfloat16)
        for h in range(HEAD_PART):
            slots[i, h * SPAN : (h + 1) * SPAN, :] = rows[:, h * HD : (h + 1) * HD]

    def target(i):
        core, seq = place(2 * dp + i // MEMBERS, i % MEMBERS)
        return core, seq, (core == dp) & (seq == s)

    def chunk(ref, a, i):
        return ref.at[a, pl.ds(pl.multiple_of(i * CHUNK, 16), CHUNK), :]

    def route(a):
        def start(n, _):
            i = (n + s) % SEQ
            core, seq, own = target(i)

            @pl.when(jnp.logical_not(own))
            def _():
                remote(
                    chunk(slots, a, i), chunk(arrived, a, s), route_send.at[a], route_recv.at[a], (core, seq, x)
                ).start()

            @pl.when(own)
            def _():
                pltpu.make_async_copy(chunk(slots, a, i), chunk(arrived, a, s), route_recv.at[a]).start()

            return 0

        lax.fori_loop(0, SEQ, start, 0)

    to_slots(0, k_ref)
    pl.semaphore_wait(barrier, 2 * SEQ - 1 + 6)
    exchange = remote(enc_ref, other, enc_sem.at[0], enc_sem.at[1], sibling)
    exchange.start()
    route(0)
    for a, ref in ((1, v_ref), (2, q_ref), (3, g_ref)):
        to_slots(a, ref)
        route(a)


    exchange.wait()
    codes[...] = jnp.where(same, enc_ref[...], other[...])

    def unit_codes(u):
        return codes[pl.ds((UNITS * me + u) % SEQ, 1), :]

    wide_iota = lax.broadcasted_iota(jnp.int32, (SHARE, 128), 1).astype(jnp.float32)
    index = []
    for u in range(UNITS):
        code = unit_codes(u)
        code = (code >> 3) * CHUNK + u * SLOTS + (code & 7)
        index.append(code)
        wide = jnp.broadcast_to(code.astype(jnp.float32), (SHARE, 128)).T
        for c in range(FLAT // 128):
            pick[u * SHARE : (u + 1) * SHARE, c * 128 : (c + 1) * 128] = one_hot(wide == wide_iota + c * 128.0)
    index = jnp.concatenate(index, axis=1)

    own_rows = pl.ds(pl.multiple_of(me * ROWS, 256), ROWS)

    def to_dense(a):
        remote(slots.at[a], arrived.at[a], route_send.at[a], route_recv.at[a], sibling).wait_recv()
        rows = jnp.dot(pick[...], arrived[a], preferred_element_type=jnp.float32)
        if a % 2 == 0:
            raw[a // 2] = rows.astype(jnp.bfloat16)
            gain = (gain_k_ref, gain_q_ref)[a // 2][...]
            rows = rows * inverse_norm(rows) * gain
        full[a, own_rows, :] = rows.astype(jnp.bfloat16)


    def member_needs(member, head):
        return ((UNITS * member) // SEQ <= head) & (head <= (UNITS * member + UNITS - 1) // SEQ)

    def device(c):
        core, seq = place(group, 2 * c + dp)
        return (core, seq, x)

    def segment(phase, member, first, count):
        return full.at[2 * phase : 2 * phase + 2, pl.ds(pl.multiple_of(member * ROWS + first, 256), count), :]

    def lane(core):
        return True if core is None else dp == core

    def other_lane(core):
        return True if core is None else dp != core

    def reached(path):
        chips = list(path[5])
        if path[7] is not None:
            chips.append(path[7])
        return chips

    def pair(phase, member):
        rows = segment(phase, member, 0, ROWS)
        return remote(rows, rows, pair_send.at[phase], pair_recv.at[phase], sibling)

    def path_copy(phase, n, member, to, send_sem):
        _, _, first, count, *_ = PATHS[n]
        rows = segment(phase, member, first, count)
        return remote(rows, rows, send_sem, path_recv.at[phase, n], device(to))

    def hand_copy(phase, n, member):
        _, _, first, count, *_ = PATHS[n]
        rows = segment(phase, member, first, count)
        return remote(rows, rows, hand_send.at[phase, n], hand_recv.at[phase, n], sibling)

    def gather_start(phase):
        for n, (c, core, _, _, _, direct, _, _) in enumerate(PATHS):

            @pl.when((chip == c) & lane(core))
            def _():
                for i, to in enumerate(direct):
                    path_copy(phase, n, me, to, path_send.at[phase, n, i]).start()

        pair(phase, me).start()

    def gather_pass(phase):
        for n, path in enumerate(PATHS):
            c, core, _, _, head, _, via, to = path
            member = 2 * c + dp

            @pl.when(among(chip, reached(path)) & lane(core))
            def _():
                path_copy(phase, n, member, c, path_send.at[phase, n, 0]).wait_recv()
                if via is not None:

                    @pl.when(chip == via)
                    def _():
                        path_copy(phase, n, member, to, pass_send.at[phase, n]).start()

                @pl.when(member_needs(2 * chip + 1 - dp, head))
                def _():
                    hand_copy(phase, n, member).start()

    def gather_finish(phase):
        pair(phase, 2 * chip + 1 - dp).wait_recv()
        for n, path in enumerate(PATHS):
            c, core, _, _, head, *_ = path

            @pl.when(among(chip, reached(path)) & other_lane(core) & member_needs(me, head))
            def _():
                hand_copy(phase, n, 2 * c + 1 - dp).wait_recv()

    def gather_sent(phase):
        pair(phase, me).wait_send()
        for n, path in enumerate(PATHS):
            c, core, _, _, head, direct, via, to = path
            member = 2 * c + dp

            @pl.when((chip == c) & lane(core))
            def _():
                for i, chip_to in enumerate(direct):
                    path_copy(phase, n, me, chip_to, path_send.at[phase, n, i]).wait_send()

            @pl.when(among(chip, reached(path)) & lane(core))
            def _():
                if via is not None:

                    @pl.when(chip == via)
                    def _():
                        path_copy(phase, n, member, to, pass_send.at[phase, n]).wait_send()

                @pl.when(member_needs(2 * chip + 1 - dp, head))
                def _():
                    hand_copy(phase, n, member).wait_send()

    to_dense(0)
    to_dense(1)
    gather_start(0)
    to_dense(2)
    to_dense(3)
    gather_start(1)
    gather_pass(0)
    gather_finish(0)


    terms[...] = jnp.zeros_like(terms)
    chunks = [slice(i * step, (i + 1) * step) for i in range(KEPT // step)]

    def tile_head(t):
        return (UNITS * me + 2 * t) // SEQ

    def head_rows(a, t, cols):
        first = tile_head(t) * KEPT + cols.start
        return full[a, pl.ds(pl.multiple_of(first, step), step), :]

    def tile_rows(a, t):
        return full[a, pl.ds(pl.multiple_of(me * ROWS + t * TILE, TILE), TILE), :]

    def query_tile(t, _):
        query, grad = tile_rows(2, t), tile_rows(3, t)
        top = None
        for cols in chunks:
            scores = lax.dot_general(query, head_rows(0, t, cols), NT, preferred_element_type=jnp.float32)
            scores = scores * (SCALING * LOG2E)
            scores_ref[:, cols] = scores
            part = lane_fold(scores, jnp.maximum)
            top = part if top is None else jnp.maximum(top, part)
        top = jnp.max(top, axis=-1, keepdims=True)
        total = jnp.zeros((TILE, 128), jnp.float32)
        weighted = jnp.zeros((TILE, 128), jnp.float32)
        for cols in chunks:
            weights = jnp.exp2(scores_ref[:, cols] - top)
            dots = lax.dot_general(grad, head_rows(1, t, cols), NT, preferred_element_type=jnp.float32)
            scores_ref[:, cols] = weights
            dots_ref[:, cols] = dots
            total += lane_fold(weights, jnp.add)
            weighted += lane_fold(weights * dots, jnp.add)
        total = jnp.sum(total, axis=-1, keepdims=True)
        share = 1.0 / total
        delta = jnp.sum(weighted, axis=-1, keepdims=True) * share
        result = jnp.zeros((TILE, HD), jnp.float32)
        for cols in chunks:
            dscore = (scores_ref[:, cols] * share) * (dots_ref[:, cols] - delta)
            result += jnp.dot(dscore.astype(jnp.bfloat16), head_rows(0, t, cols), preferred_element_type=jnp.float32)
        rows = pl.ds(pl.multiple_of(t * TILE, TILE), TILE)
        grads, term = norm_grads(raw[1, rows, :], gain_q_ref[...], result * SCALING)
        q_grad[rows, :] = grads.astype(jnp.bfloat16)
        terms[0:8, :] += term
        for i, value in enumerate((top + jnp.log2(total), delta)):
            wide = jnp.broadcast_to(value, (TILE, 128)).T
            for j in range(TILE // SHARE):
                stats[me, i, pl.ds(2 * t + j, 1), :] = wide[0:1, j * SHARE : (j + 1) * SHARE]

        @pl.when(t == 1)
        def _():
            gather_pass(1)

        return 0

    lax.fori_loop(0, TILES, query_tile, 0)


    def shares(member):
        return (
            ((UNITS * member) // SEQ <= (UNITS * me + UNITS - 1) // SEQ)
            & ((UNITS * me) // SEQ <= (UNITS * member + UNITS - 1) // SEQ)
            & (member != me)
        )

    def stat_copy(member, dst):
        core, seq = place(group, member)
        return remote(stats.at[me], stats.at[dst], stat_send.at[member], stat_recv.at[dst], (core, seq, x))

    def stat_start(i, _):
        @pl.when(shares(i))
        def _():
            stat_copy(i, me).start()

        return 0

    def stat_finish(i, _):
        @pl.when(shares(i))
        def _():
            stat_copy(i, i).wait_recv()
            stat_copy(i, me).wait_send()

        return 0

    lax.fori_loop(0, MEMBERS, stat_start, 0)


    def to_self(i):
        return same & (i == s)

    flat_iota = lax.broadcasted_iota(jnp.int32, (step, ROWS), 0)
    for c in range(FLAT // step):
        spread = one_hot(flat_iota + c * step == index)
        rows = jnp.dot(spread, q_grad[...], preferred_element_type=jnp.float32)
        q_slots[c * step : (c + 1) * step, :] = rows.astype(jnp.bfloat16)

    def q_home(i):
        return (
            q_slots.at[pl.ds(pl.multiple_of(i * CHUNK, 16), CHUNK), :],
            home_ref.at[0, pl.ds(pl.multiple_of(seat * CHUNK, 16), CHUNK), :],
        )

    def q_home_start(n, _):
        i = (n + s) % SEQ
        src, dst = q_home(i)

        @pl.when(jnp.logical_not(to_self(i)))
        def _():
            remote(src, dst, home_send.at[0], home_recv.at[0], (clip, i, x)).start()

        @pl.when(to_self(i))
        def _():
            pltpu.make_async_copy(src, dst, home_recv.at[0]).start()

        return 0

    lax.fori_loop(0, SEQ, q_home_start, 0)


    gather_finish(1)
    lax.fori_loop(0, MEMBERS, stat_finish, 0)
    tile_iota = lax.broadcasted_iota(jnp.int32, (2 * SLOTS * SEQ, TILE), 0)

    def stat_row(i, t, cols):
        first = tile_head(t) * SEQ + cols.start // SHARE
        pieces = []
        for j in range(step // SHARE):
            unit = first + j
            pieces.append(stats[unit // UNITS, i, pl.ds(unit % UNITS, 1), :])
        return jnp.concatenate(pieces, axis=1)

    def kv_home(t, i):
        return (
            kv_slots.at[t, :, pl.ds(pl.multiple_of(i * 2 * SLOTS, 16), 2 * SLOTS), :],
            home_ref.at[1:3, pl.ds(pl.multiple_of(seat * CHUNK + t * 2 * SLOTS, 16), 2 * SLOTS), :],
        )

    def key_tile(t, _):
        key, value = tile_rows(0, t), tile_rows(1, t)
        key_grad = jnp.zeros((TILE, HD), jnp.float32)
        value_grad = jnp.zeros((TILE, HD), jnp.float32)
        for cols in chunks:
            query, grad = head_rows(2, t, cols), head_rows(3, t, cols)
            scores = lax.dot_general(key, query, NT, preferred_element_type=jnp.float32)
            weights = jnp.exp2(scores * (SCALING * LOG2E) - stat_row(0, t, cols))
            dots = lax.dot_general(value, grad, NT, preferred_element_type=jnp.float32)
            dscore = weights * (dots - stat_row(1, t, cols))
            key_grad += jnp.dot(dscore.astype(jnp.bfloat16), query, preferred_element_type=jnp.float32)
            value_grad += jnp.dot(weights.astype(jnp.bfloat16), grad, preferred_element_type=jnp.float32)
        rows = pl.ds(pl.multiple_of(t * TILE, TILE), TILE)
        grads, term = norm_grads(raw[0, rows, :], gain_k_ref[...], key_grad * SCALING)
        terms[8:16, :] += term
        tile_codes = []
        for j in range(2):
            code = unit_codes(2 * t + j)
            tile_codes.append((code >> 3) * (2 * SLOTS) + j * SLOTS + (code & 7))
        spread = one_hot(tile_iota == jnp.concatenate(tile_codes, axis=1))
        for i, result in enumerate((grads, value_grad)):
            result = jnp.dot(spread, result.astype(jnp.bfloat16), preferred_element_type=jnp.float32)
            kv_slots[t, i] = result.astype(jnp.bfloat16)

        def start(n, _):
            i = (n + s) % SEQ
            src, dst = kv_home(t, i)

            @pl.when(jnp.logical_not(to_self(i)))
            def _():
                remote(src, dst, home_send.at[1], home_recv.at[1], (clip, i, x)).start()

            @pl.when(to_self(i))
            def _():
                pltpu.make_async_copy(src, dst, home_recv.at[1]).start()

            return 0

        lax.fori_loop(0, SEQ, start, 0)
        return 0

    lax.fori_loop(0, TILES, key_tile, 0)


    def part_start(i, _):
        @pl.when(jnp.logical_not(to_self(i)))
        def _():
            remote(terms, parts.at[seat], part_sem.at[0], part_sem.at[1], (clip, i, x)).start()

        @pl.when(to_self(i))
        def _():
            pltpu.make_async_copy(terms, parts.at[seat], part_sem.at[1]).start()

        return 0

    lax.fori_loop(0, SEQ, part_start, 0)
    remote(parts, parts, part_sem.at[0], part_sem.at[1], sibling).wait_recv()
    partial[...] = jnp.sum(parts[...], axis=0)

    def cross_copy(i, dst):
        return remote(partial, cross.at[dst], cross_send.at[i], cross_recv.at[dst], (i // 4, s, i % 4))

    def cross_start(i, _):
        @pl.when(i != corner)
        def _():
            cross_copy(i, corner).start()

        return 0

    def cross_finish(i, _):
        @pl.when(i != corner)
        def _():
            cross_copy(i, i).wait_recv()
            cross_copy(i, corner).wait_send()

        return 0

    cross[pl.ds(corner, 1)] = partial[...][None]
    lax.fori_loop(0, 8, cross_start, 0)
    lax.fori_loop(0, 8, cross_finish, 0)
    total_ref[...] = jnp.sum(cross[...], axis=0)


    @pl.when(same)
    def _():
        most = SEQ - 1
        for a in range(4):
            rows = slots.at[a, 0 : most * CHUNK, :]
            remote(rows, rows, route_send.at[a], route_recv.at[a], sibling).wait_send()
        rows = q_slots.at[0 : most * CHUNK, :]
        remote(rows, rows, home_send.at[0], home_recv.at[0], sibling).wait_send()
        rows = kv_slots.at[:, :, 0 : most * 2 * SLOTS, :]
        remote(rows, rows, home_send.at[1], home_recv.at[1], sibling).wait_send()
        rows = parts.at[0:most]
        remote(rows, rows, part_sem.at[0], part_sem.at[1], sibling).wait_send()

    @pl.when(jnp.logical_not(same))
    def _():
        for a in range(4):
            remote(slots.at[a], slots.at[a], route_send.at[a], route_recv.at[a], sibling).wait_send()
        remote(q_slots, q_slots, home_send.at[0], home_recv.at[0], sibling).wait_send()
        remote(kv_slots, kv_slots, home_send.at[1], home_recv.at[1], sibling).wait_send()
        remote(parts, parts, part_sem.at[0], part_sem.at[1], sibling).wait_send()

    gather_sent(0)
    gather_sent(1)
    remote(q_slots, home_ref.at[0], home_send.at[0], home_recv.at[0], sibling).wait_recv()
    remote(home_ref.at[1:3], home_ref.at[1:3], home_send.at[1], home_recv.at[1], sibling).wait_recv()


def core(slot_row, token_row, enc, k, v, q, g, gain_q, gain_k):
    bf16, f32 = jnp.bfloat16, jnp.float32
    dma = pltpu.SemaphoreType.DMA
    paths = len(PATHS)
    in_vmem = pl.BlockSpec(memory_space=pltpu.VMEM)
    return pl.pallas_call(
        core_kernel,
        name="core",
        in_specs=[in_vmem] * 9,
        out_specs=[pl.BlockSpec(memory_space=pl.ANY), in_vmem, in_vmem],
        out_shape=(
            jax.ShapeDtypeStruct((3, FLAT, HD), bf16),
            jax.ShapeDtypeStruct((SPAN, SPAN), bf16),
            jax.ShapeDtypeStruct((16, HD), f32),
        ),
        scratch_shapes=[
            pltpu.VMEM((4, FLAT, HD), bf16),
            pltpu.VMEM((4, FLAT, HD), bf16),
            pltpu.VMEM((SEQ, SHARE), jnp.int32),
            pltpu.VMEM((SEQ, SHARE), jnp.int32),
            pltpu.VMEM((ROWS, FLAT), bf16),
            pltpu.VMEM((4, MEMBERS * ROWS, HD), bf16),
            pltpu.VMEM((2, ROWS, HD), bf16),
            pltpu.VMEM((TILE, KEPT), f32),
            pltpu.VMEM((TILE, KEPT), f32),
            pltpu.VMEM((ROWS, HD), bf16),
            pltpu.VMEM((FLAT, HD), bf16),
            pltpu.VMEM((TILES, 2, 2 * SLOTS * SEQ, HD), bf16),
            pltpu.VMEM((MEMBERS, 2, 8, SHARE), f32),
            pltpu.VMEM((16, HD), f32),
            pltpu.VMEM((SEQ, 16, HD), f32),
            pltpu.VMEM((16, HD), f32),
            pltpu.VMEM((8, 16, HD), f32),
            dma((2,)),
            dma((4,)),
            dma((4,)),
            dma((2,)),
            dma((2,)),
            dma((2, paths, 3)),
            dma((2, paths)),
            dma((2, paths)),
            dma((2, paths)),
            dma((2, paths)),
            dma((MEMBERS,)),
            dma((MEMBERS,)),
            dma((2,)),
            dma((2,)),
            dma((2,)),
            dma((8,)),
            dma((8,)),
        ],
        compiler_params=pltpu.CompilerParams(
            collective_id=0, has_side_effects=True, vmem_limit_bytes=VMEM_LIMIT
        ),
    )(slot_row, token_row, enc, k, v, q, g, gain_q, gain_k)


def rows_kernel(back_ref, slots_ref, total_ref, q_ref, k_ref, v_ref, gain_q_ref, gain_k_ref):
    for i, ref in enumerate((q_ref, k_ref, v_ref)):
        ref[0] = jnp.dot(back_ref[...], slots_ref[i], preferred_element_type=jnp.float32).astype(jnp.bfloat16)
    gain_q_ref[...] = jnp.sum(total_ref[0:8, :], axis=0, keepdims=True)
    gain_k_ref[...] = jnp.sum(total_ref[8:16, :], axis=0, keepdims=True)


def to_rows(back, slots, total):
    width = HEAD_PART * HD
    big = jax.ShapeDtypeStruct((1, SPAN, width), jnp.bfloat16)
    small = jax.ShapeDtypeStruct((1, HD), jnp.float32)
    return pl.pallas_call(
        rows_kernel,
        name="to_rows",
        grid=(HEAD_PART,),
        in_specs=[
            pl.BlockSpec((SPAN, SPAN), lambda h: (0, 0)),
            pl.BlockSpec((3, SPAN, HD), lambda h: (0, h, 0)),
            pl.BlockSpec((16, HD), lambda h: (0, 0)),
        ],
        out_specs=[pl.BlockSpec((1, SPAN, HD), lambda h: (0, 0, h))] * 3 + [pl.BlockSpec((1, HD), lambda h: (0, 0))] * 2,
        out_shape=(big, big, big, small, small),
        cost_estimate=pl.CostEstimate(flops=3 * 10**8, bytes_accessed=3 * 10**6, transcendentals=0),
    )(back, slots, total)


def on_device(q_raw, k_raw, v_raw, out_grad, gain_q, gain_k, keep_list):
    s = lax.axis_index("seq")
    listing = keep_list[0].reshape(SEQ, SHARE)
    source = listing // SPAN
    hits = source[None] == jnp.arange(SEQ, dtype=jnp.int32)[:, None, None]
    earlier = jnp.triu(jnp.ones((SHARE, SHARE), jnp.bfloat16), 1)
    counts = jnp.dot(hits.astype(jnp.bfloat16), earlier, preferred_element_type=jnp.float32)
    rank = jnp.sum(jnp.where(hits, counts, 0.0), axis=0).astype(jnp.int32)
    slot = jnp.arange(SEQ, dtype=jnp.int32)[:, None] * SLOTS + rank
    slot_row = jnp.where(source == s, slot, -1).reshape(1, KEPT)
    token_row = (listing - s * SPAN).reshape(1, KEPT)
    enc = source * SLOTS + rank
    home, back, total = core(
        slot_row,
        token_row,
        enc,
        k_raw[0],
        v_raw[0],
        q_raw[0],
        out_grad[0],
        gain_q.reshape(1, HD),
        gain_k.reshape(1, HD),
    )
    q_out, k_out, v_out, gain_q_grad, gain_k_grad = to_rows(back, home, total)
    return q_out, k_out, v_out, gain_q_grad.reshape(HD), gain_k_grad.reshape(HD)


def solution(mesh):
    big = P("dp", "seq", "tensor")
    return jax.shard_map(
        on_device,
        mesh=mesh,
        in_specs=(big, big, big, big, P(), P(), P("dp", None)),
        out_specs=(big, big, big, P(), P()),
        check_vma=False,
    )
```

time: 917 us -> 154 us (0.17); the launches traced: 903 us -> 154 us
  blocking collectives: 299 us -> 0 us
  waiting for transfers between devices: 244 us -> 0 us
  matrix products: 158 us -> 0.25 us
  Pallas kernels: 0 us -> 149 us
  local copies, waits for them, and re-layouts: 140 us -> 0 us
  starting transfers between devices: 29.8 us -> 0 us
  between operations: 15.6 us -> 0.66 us
  other arithmetic: 14.1 us -> 3.49 us
    all_gather x8 -> x0, waiting for transfers between devices: 223 us -> none  [the longest x2 90 us: key_side(): lax.all_gather(value_rows.reshape(row_count, flat_width), 'seq', axis=0,...]
    all_gather x4 -> x0, blocking collectives: 160 us -> none  [the longest x2 82.3 us: key_side(): lax.all_gather(log_norm, 'seq', axis=1, tiled=True)]
    dot_general x112 -> x1, matrix products: 158 us -> 0.25 us  [on_device(): jnp.dot(hits.astype(jnp.bfloat16), earlier, preferred_element_type=jnp.fl...]
    pallas_call x0 -> x2, Pallas kernels: none -> 149 us  [the longest x1 144 us: core(): pl.pallas_call(core_kernel, name='core', in_specs=[in_vmem] * 9, out_spec...]
    psum x1 -> x0, blocking collectives: 81.7 us -> none  [on_device(): lax.psum((term_q, term_k), ('dp', 'seq', 'tensor'))]
    unnamed x118 -> x0, local copies, waits for them, and re-layouts: 60.1 us -> none
    all_to_all x3 -> x0, blocking collectives: 57.4 us -> none  [the longest x1 20.4 us: on_device(): lax.all_to_all(send_g, 'seq', split_axis=0, concat_axis=0, tiled=True)]
    scatter x6 -> x0, local copies, waits for them, and re-layouts: 40.8 us -> none  [the longest x2 31 us: on_device(): jnp.zeros((seq_count * slot_count,), jnp.int32).at[target]]
  transfers between devices with their start and end apart: 12 -> 0, of which waited for: 8 -> 0; matrix products, arithmetic and copies ran while one was open for 28% -> 0% of each run, Pallas kernels for 0% -> 0%
where the time goes in v1:
time: 154 us
  Pallas kernels  149 us (97%)
  other arithmetic  3.49 us (2%)
    pallas_call x1, Pallas kernels, core(): pl.pallas_call(core_kernel, name='core', in_specs=[in_vmem] * 9, out_spec...  144 us
    pallas_call x1, Pallas kernels, to_rows(): pl.pallas_call(rows_kernel, name='to_rows', grid=(HEAD_PART,), in_specs=[...  5.04 us

profile of v1, /device:TPU:1, one launch (start us, length us, event | category | flops | bytes accessed | tf_op | source)
XLA Modules:
  0.0 153.5 jit_solution(18207219763030002762)
XLA Ops:
  0.6 0.7 add_select_fusion
  1.4 0.2 fusion
  1.6 1.3 multiply_add_fusion
  3.0 1.4 broadcast_subtract_fusion
  4.4 144.1 %core.1 = (bf16[3,1536,128]{2,1,0:T(8,128)(2,1)}, bf16[256,256]{1,0:T(8,128)(2,1)}, f32[16,128]{1,0:T(8,128)}) custom-call(s32[1,4096]{1,0:T(1,128)} %get-tuple-element.24.slot_ref, s32[1,4096]{1,0:T(1,128)} %get-tuple-element.23.row_ref, s32[32,128]{1,0:T(8,128)} %get-tuple-element.21.enc_ref, bf16[256,768]{1,0:T(8,128)(2,1)} %bitcast.13, ...), custom_call_target="tpu_custom_call" | custom-call | tf_op jit(solution)/shard_map/core/pallas_call | solution.py:623
  148.5 5.0 %to_rows.1 = (bf16[1,256,768]{2,1,0:T(8,128)(2,1)}, bf16[1,256,768]{2,1,0:T(8,128)(2,1)}, bf16[1,256,768]{2,1,0:T(8,128)(2,1)}, f32[1,128]{1,0:T(1,128)}, f32[1,128]{1,0:T(1,128)}) custom-call(bf16[256,256]{1,0:T(8,128)(2,1)} %get-tuple-element.13.back_ref, bf16[3,1536,128]{2,1,0:T(8,128)(2,1)} %get-tuple-element.14.slots_ref, ...), custom_call_target="tpu_custom_call" | custom-call | flops 300000000 | bytes 3000000 | tf_op jit(solution)/shard_map/to_rows/pallas_call | solution.py:686
  (1 shorter events, 0.0 us)

commit v2 on v1

v2 whole, which is shorter than its diff:
```python
import math

import jax
import jax.numpy as jnp
from jax import lax
from jax.experimental import pallas as pl
from jax.experimental.pallas import tpu as pltpu
from jax.sharding import PartitionSpec as P

MESH = pl.DeviceIdType.MESH
HD = 128
EPSILON = 1e-06
SEQ = 32
SPAN = 256
SHARE = 128
SLOTS = 8
HEAD_PART = 6
UNITS = 6
ROWS = UNITS * SHARE
CHUNK = UNITS * SLOTS
FLAT = SEQ * CHUNK
MEMBERS = 16
KEPT = SEQ * SHARE
TILE = 256
TILES = ROWS // TILE
SCALING = 1.0 / math.sqrt(HD)
LOG2E = 1.4426950408889634
VMEM_LIMIT = 56 * 1024 * 1024

NT = (((1,), (1,)), ((), ()))

PATHS = (
    (0, None, 0, 768, 0, (1,), 1, 2),
    (1, None, 0, 768, 0, (2, 0), None, None),
    (2, 0, 0, 768, 0, (1,), 1, 0),
    (2, 1, 0, 256, 0, (1,), 1, 0),
    (2, 1, 256, 512, 1, (3, 5), 5, 4),
    (3, 0, 0, 768, 1, (2, 4), 2, 5),
    (3, 1, 0, 768, 1, (4, 2), 4, 5),
    (4, 0, 0, 768, 1, (5, 3), 5, 2),
    (4, 1, 0, 768, 1, (3, 5), 3, 2),
    (5, 0, 0, 512, 1, (4, 2), 2, 3),
    (5, 0, 512, 256, 2, (6,), 6, 7),
    (5, 1, 0, 768, 2, (6,), 6, 7),
    (6, None, 0, 768, 2, (5, 7), None, None),
    (7, None, 0, 768, 2, (6,), 6, 5),
)


def place(x, clip, third, member):
    chip, core = member >> 1, member & 1
    dz = chip >> 2
    turn = chip ^ (7 * dz)
    dx = turn >> 1
    dy = dx ^ (turn & 1)
    y = 2 * (x & 1) + dy
    z = 4 * clip + 2 * third + dz
    return core, y * 8 + z, (x & 2) + dx


def my_place(dp, s, x):
    y, z = s >> 3, s & 7
    dx, dy, dz = x & 1, y & 1, z & 1
    turn = 2 * dx + (dx ^ dy)
    return (x & 2) + (y >> 1), z >> 2, (z >> 1) & 1, turn ^ (7 * dz)


def among(value, options):
    hit = value == options[0]
    for option in options[1:]:
        hit = hit | (value == option)
    return hit


def one_hot(hit):
    return jnp.where(hit, 1.0, 0.0).astype(jnp.bfloat16)


def inverse_norm(x):
    return lax.rsqrt(jnp.mean(x * x, axis=-1, keepdims=True) + EPSILON)


def norm_grads(raw, gain, upstream):
    raw = raw.astype(jnp.float32)
    inverse = inverse_norm(raw)
    scaled = upstream * gain
    inner = jnp.mean(scaled * raw, axis=-1, keepdims=True)
    grads = inverse * scaled - raw * (inverse * inverse * inverse * inner)
    terms = upstream * raw * inverse
    return grads, jnp.sum(terms.reshape(-1, 8, HD), axis=0)


def lane_fold(x, fold):
    parts = [x[:, i * 128 : (i + 1) * 128] for i in range(x.shape[1] // 128)]
    total = parts[0]
    for part in parts[1:]:
        total = fold(total, part)
    return total


def core_kernel(
    list_ref,
    k_ref,
    q_ref,
    v_ref,
    g_ref,
    gain_q_ref,
    gain_k_ref,
    home_ref,
    back_ref,
    total_ref,
    slots,
    arrived,
    enc_ref,
    other,
    codes,
    pick,
    full,
    raw,
    scores_ref,
    dots_ref,
    sums,
    q_grad,
    q_slots,
    kv_slots,
    stats,
    flat_stats,
    terms,
    parts,
    partial,
    cross,
    enc_sem,
    route_send,
    route_recv,
    pair_send,
    pair_recv,
    path_send,
    path_recv,
    pass_send,
    hand_send,
    hand_recv,
    stat_send,
    stat_recv,
    home_send,
    home_recv,
    part_sem,
    cross_send,
    cross_recv,
):
    dp, s, x = lax.axis_index("dp"), lax.axis_index("seq"), lax.axis_index("tensor")
    head_x, clip, third, chip = my_place(dp, s, x)
    me = 2 * chip + dp
    seat = third * MEMBERS + me
    sibling = (1 - dp, s, x)
    corner = dp * 4 + x
    same = (clip == dp) & (head_x == x)

    own_source = jnp.where(same, s, -1)

    def to_self(i):
        return i == own_source

    own_target = jnp.where(same, seat, -1)

    def target(i):
        return place(x, dp, i >> 4, i & 15), i == own_target

    def source(i):
        return (clip, i, head_x)

    def device(c):
        return place(head_x, clip, third, 2 * c + dp)

    def remote(src, dst, send_sem, recv_sem, device):
        return pltpu.make_async_remote_copy(
            src_ref=src, dst_ref=dst, send_sem=send_sem, recv_sem=recv_sem, device_id=device, device_id_type=MESH
        )


    barrier = pltpu.get_barrier_semaphore()

    def greet_device(there):
        pl.semaphore_signal(barrier, inc=1, device_id=there, device_id_type=MESH)

    def greet(i, _):
        there, own = target(i)

        @pl.when(jnp.logical_not(own))
        def _():
            greet_device(there)

        @pl.when(jnp.logical_not(to_self(i)))
        def _():
            greet_device(source(i))

        return 0

    lax.fori_loop(0, SEQ, greet, 0)

    def greet_near(i, _):
        @pl.when(i != corner)
        def _():
            greet_device((i >> 2, s, i & 3))

        @pl.when(i != chip)
        def _():
            greet_device(device(i))

        return 0

    lax.fori_loop(0, 8, greet_near, 0)
    greet_device(sibling)


    listing = list_ref[...]
    from_block = listing >> 8
    hits = one_hot(jnp.concatenate([from_block == i for i in range(SEQ)], axis=0))
    earlier = lax.broadcasted_iota(jnp.int32, (SHARE, SHARE), 0) < lax.broadcasted_iota(jnp.int32, (SHARE, SHARE), 1)
    counts = jnp.dot(hits, one_hot(earlier), preferred_element_type=jnp.float32) * hits.astype(jnp.float32)
    rank = counts[0:SEQ]
    for i in range(1, SEQ):
        rank += counts[i * SEQ : (i + 1) * SEQ]
    rank = rank.astype(jnp.int32)
    enc_ref[...] = from_block * SLOTS + rank
    slot = lax.broadcasted_iota(jnp.int32, (SEQ, SHARE), 0) * SLOTS + rank
    slot = jnp.where(from_block == s, slot, -1)
    token = listing - s * SPAN

    def lanes(x, c):
        return jnp.concatenate([x[j : j + 1] for j in range(c * step // SHARE, (c + 1) * step // SHARE)], axis=1)

    step = 512
    iota = lax.broadcasted_iota(jnp.int32, (SPAN, step), 0)
    take = jnp.zeros((SPAN, SPAN), jnp.float32)
    back = jnp.zeros((SPAN, SPAN), jnp.float32)
    for c in range(KEPT // step):
        a = one_hot(iota == lanes(slot, c))
        b = one_hot(iota == lanes(token, c))
        take += lax.dot_general(a, b, NT, preferred_element_type=jnp.float32)
        back += lax.dot_general(b, a, NT, preferred_element_type=jnp.float32)
    take = take.astype(jnp.bfloat16)
    back_ref[...] = back.astype(jnp.bfloat16)

    def to_slots(i, ref):
        rows = jnp.dot(take, ref[...], preferred_element_type=jnp.float32).astype(jnp.bfloat16)
        for h in range(HEAD_PART):
            slots[i, h * SPAN : (h + 1) * SPAN, :] = rows[:, h * HD : (h + 1) * HD]

    def chunk(ref, a, i):
        return ref.at[a, pl.ds(pl.multiple_of(i * CHUNK, 16), CHUNK), :]

    def route(a):
        def start(n, _):
            i = (n + s) & (SEQ - 1)
            there, own = target(i)

            @pl.when(jnp.logical_not(own))
            def _():
                remote(chunk(slots, a, i), chunk(arrived, a, s), route_send.at[a], route_recv.at[a], there).start()

            return 0

        lax.fori_loop(0, SEQ, start, 0)

        @pl.when(same)
        def _():
            pltpu.make_async_copy(chunk(slots, a, seat), chunk(arrived, a, s), route_recv.at[a]).start()

    to_slots(0, k_ref)
    pl.semaphore_wait(barrier, 2 * SEQ + 15 - 2 * same.astype(jnp.int32))
    exchange = remote(enc_ref, other, enc_sem.at[0], enc_sem.at[1], sibling)
    exchange.start()
    route(0)
    to_slots(1, q_ref)
    route(1)
    to_slots(2, v_ref)
    route(2)
    to_slots(3, g_ref)


    exchange.wait()
    codes[...] = jnp.where(clip == dp, enc_ref[...], other[...])

    def unit_codes(u):
        return codes[pl.ds((UNITS * me + u) & (SEQ - 1), 1), :]

    wide_iota = lax.broadcasted_iota(jnp.int32, (SHARE, 128), 1).astype(jnp.float32)
    index = []
    for u in range(UNITS):
        code = unit_codes(u)
        code = (code >> 3) * CHUNK + u * SLOTS + (code & 7)
        index.append(code)
        wide = jnp.broadcast_to(code.astype(jnp.float32), (SHARE, 128)).T
        for c in range(FLAT // 128):
            pick[u * SHARE : (u + 1) * SHARE, c * 128 : (c + 1) * 128] = one_hot(wide == wide_iota + c * 128.0)
    index = jnp.concatenate(index, axis=1)

    own_rows = pl.ds(pl.multiple_of(me * ROWS, 256), ROWS)

    def to_dense(a):
        remote(slots.at[a], arrived.at[a], route_send.at[a], route_recv.at[a], sibling).wait_recv()
        rows = jnp.dot(pick[...], arrived[a], preferred_element_type=jnp.float32)
        if a < 2:
            raw[a] = rows.astype(jnp.bfloat16)
            gain = (gain_k_ref, gain_q_ref)[a][...]
            rows = rows * inverse_norm(rows) * gain
        full[a, own_rows, :] = rows.astype(jnp.bfloat16)


    def heads_of(member):
        return (UNITS * member) >> 5, (UNITS * member + UNITS - 1) >> 5

    my_heads, pair_heads = heads_of(me), heads_of(2 * chip + 1 - dp)

    def have(heads, head):
        return (heads[0] <= head) & (head <= heads[1])

    def segment(phase, member, first, count):
        return full.at[phase, pl.ds(pl.multiple_of(member * ROWS + first, 256), count), :]

    def lane(core):
        return True if core is None else dp == core

    def other_lane(core):
        return True if core is None else dp != core

    def reached(path):
        chips = list(path[5])
        if path[7] is not None:
            chips.append(path[7])
        return chips

    def pair(phase, member):
        rows = segment(phase, member, 0, ROWS)
        return remote(rows, rows, pair_send.at[phase], pair_recv.at[phase], sibling)

    def path_copy(phase, n, member, to, send_sem):
        _, _, first, count, *_ = PATHS[n]
        rows = segment(phase, member, first, count)
        return remote(rows, rows, send_sem, path_recv.at[phase, n], device(to))

    def hand_copy(phase, n, member):
        _, _, first, count, *_ = PATHS[n]
        rows = segment(phase, member, first, count)
        return remote(rows, rows, hand_send.at[phase, n], hand_recv.at[phase, n], sibling)

    def gather_start(phase):
        for n, (c, core, _, _, _, direct, _, _) in enumerate(PATHS):

            @pl.when((chip == c) & lane(core))
            def _():
                for i, to in enumerate(direct):
                    path_copy(phase, n, me, to, path_send.at[phase, n, i]).start()

        pair(phase, me).start()

    def gather_pass(phase):
        def take_in(n, chips, via, to):
            c, core, _, _, head, *_ = PATHS[n]
            member = 2 * c + dp

            @pl.when(among(chip, chips) & lane(core))
            def _():
                path_copy(phase, n, member, c, path_send.at[phase, n, 0]).wait_recv()
                if via is not None:

                    @pl.when(chip == via)
                    def _():
                        path_copy(phase, n, member, to, pass_send.at[phase, n]).start()

                @pl.when(have(pair_heads, head))
                def _():
                    hand_copy(phase, n, member).start()

        for n, path in enumerate(PATHS):
            take_in(n, path[5], path[6], path[7])
        for n, path in enumerate(PATHS):
            if path[7] is not None:
                take_in(n, (path[7],), None, None)

    def gather_finish(phase):
        pair(phase, 2 * chip + 1 - dp).wait_recv()
        for n, path in enumerate(PATHS):
            c, core, _, _, head, *_ = path

            @pl.when(among(chip, reached(path)) & other_lane(core) & have(my_heads, head))
            def _():
                hand_copy(phase, n, 2 * c + 1 - dp).wait_recv()

    def gather_sent(phase):
        pair(phase, me).wait_send()
        for n, path in enumerate(PATHS):
            c, core, _, _, head, direct, via, to = path
            member = 2 * c + dp

            @pl.when((chip == c) & lane(core))
            def _():
                for i, chip_to in enumerate(direct):
                    path_copy(phase, n, me, chip_to, path_send.at[phase, n, i]).wait_send()

            @pl.when(among(chip, reached(path)) & lane(core))
            def _():
                if via is not None:

                    @pl.when(chip == via)
                    def _():
                        path_copy(phase, n, member, to, pass_send.at[phase, n]).wait_send()

                @pl.when(have(pair_heads, head))
                def _():
                    hand_copy(phase, n, member).wait_send()

    to_dense(0)
    gather_start(0)
    route(3)
    to_dense(1)
    gather_pass(0)
    gather_finish(0)


    terms[...] = jnp.zeros_like(terms)
    chunks = [slice(i * step, (i + 1) * step) for i in range(KEPT // step)]

    def tile_head(t):
        return (UNITS * me + 2 * t) >> 5

    def head_rows(a, t, cols):
        first = tile_head(t) * KEPT + cols.start
        return full[a, pl.ds(pl.multiple_of(first, step), step), :]

    def tile_rows(a, t):
        return full[a, pl.ds(pl.multiple_of(me * ROWS + t * TILE, TILE), TILE), :]

    def local_rows(t):
        return pl.ds(pl.multiple_of(t * TILE, TILE), TILE)

    def store_stat(i, t, value):
        wide = jnp.broadcast_to(value, (TILE, 128)).T
        for j in range(TILE // SHARE):
            stats[me, i, pl.ds(2 * t + j, 1), :] = wide[0:1, j * SHARE : (j + 1) * SHARE]

    def score_tile(t, _):
        query = tile_rows(1, t)
        rows = local_rows(t)
        top = None
        for cols in chunks:
            scores = lax.dot_general(query, head_rows(0, t, cols), NT, preferred_element_type=jnp.float32)
            scores = scores * (SCALING * LOG2E)
            scores_ref[rows, cols] = scores
            part = lane_fold(scores, jnp.maximum)
            top = part if top is None else jnp.maximum(top, part)
        top = jnp.max(top, axis=-1, keepdims=True)
        total = jnp.zeros((TILE, 128), jnp.float32)
        for cols in chunks:
            weights = jnp.exp2(scores_ref[rows, cols] - top)
            scores_ref[rows, cols] = weights
            total += lane_fold(weights, jnp.add)
        total = jnp.sum(total, axis=-1, keepdims=True)
        sums[rows, :] = jnp.broadcast_to(total, (TILE, 128))
        store_stat(0, t, top + jnp.log2(total))

        @pl.when(t == 0)
        def _():
            to_dense(2)
            gather_start(2)
            gather_start(1)

        return 0

    lax.fori_loop(0, TILES, score_tile, 0)
    gather_pass(2)
    to_dense(3)
    gather_start(3)
    gather_finish(2)

    def query_tile(t, _):
        grad = tile_rows(3, t)
        rows = local_rows(t)
        weighted = jnp.zeros((TILE, 128), jnp.float32)
        for cols in chunks:
            dots = lax.dot_general(grad, head_rows(2, t, cols), NT, preferred_element_type=jnp.float32)
            dots_ref[:, cols] = dots
            weighted += lane_fold(scores_ref[rows, cols] * dots, jnp.add)
        share = 1.0 / sums[rows, 0:1]
        delta = jnp.sum(weighted, axis=-1, keepdims=True) * share
        result = jnp.zeros((TILE, HD), jnp.float32)
        for cols in chunks:
            dscore = (scores_ref[rows, cols] * share) * (dots_ref[:, cols] - delta)
            result += jnp.dot(dscore.astype(jnp.bfloat16), head_rows(0, t, cols), preferred_element_type=jnp.float32)
        grads, term = norm_grads(raw[1, rows, :], gain_q_ref[...], result * SCALING)
        q_grad[rows, :] = grads.astype(jnp.bfloat16)
        terms[0:8, :] += term
        store_stat(1, t, delta)

        @pl.when(t == 0)
        def _():
            gather_pass(1)

        @pl.when(t == 1)
        def _():
            gather_pass(3)

        return 0

    lax.fori_loop(0, TILES, query_tile, 0)


    def shares(member):
        first, last = heads_of(member)
        return (first <= my_heads[1]) & (my_heads[0] <= last) & (member != me)

    def stat_copy(member, dst):
        there = place(head_x, clip, third, member)
        return remote(stats.at[me], stats.at[dst], stat_send.at[member], stat_recv.at[dst], there)

    def stat_start(i, _):
        @pl.when(shares(i))
        def _():
            stat_copy(i, me).start()

        return 0

    def stat_finish(i, _):
        @pl.when(shares(i))
        def _():
            stat_copy(i, i).wait_recv()
            stat_copy(i, me).wait_send()

        return 0

    def stat_flat(i):
        @pl.when(shares(i) | (me == i))
        def _():
            flat_stats[:, i * UNITS : (i + 1) * UNITS, :] = stats[i, :, 0:UNITS, :]

    lax.fori_loop(0, MEMBERS, stat_start, 0)


    flat_iota = lax.broadcasted_iota(jnp.int32, (step, ROWS), 0)
    for c in range(FLAT // step):
        spread = one_hot(flat_iota + c * step == index)
        rows = jnp.dot(spread, q_grad[...], preferred_element_type=jnp.float32)
        q_slots[c * step : (c + 1) * step, :] = rows.astype(jnp.bfloat16)

    def q_home(i):
        return (
            q_slots.at[pl.ds(pl.multiple_of(i * CHUNK, 16), CHUNK), :],
            home_ref.at[0, pl.ds(pl.multiple_of(seat * CHUNK, 16), CHUNK), :],
        )

    def q_home_start(n, _):
        i = (n + s) & (SEQ - 1)
        src, dst = q_home(i)

        @pl.when(jnp.logical_not(to_self(i)))
        def _():
            remote(src, dst, home_send.at[0], home_recv.at[0], source(i)).start()

        return 0

    lax.fori_loop(0, SEQ, q_home_start, 0)

    @pl.when(same)
    def _():
        src, dst = q_home(s)
        pltpu.make_async_copy(src, dst, home_recv.at[0]).start()


    gather_finish(1)
    gather_finish(3)
    lax.fori_loop(0, MEMBERS, stat_finish, 0)
    for i in range(MEMBERS):
        stat_flat(i)
    tile_iota = lax.broadcasted_iota(jnp.int32, (2 * SLOTS * SEQ, TILE), 0)

    def stat_row(i, t, cols):
        first = tile_head(t) * SEQ + cols.start // SHARE
        return jnp.concatenate([flat_stats[i, pl.ds(first + j, 1), :] for j in range(step // SHARE)], axis=1)

    def kv_home(t, i):
        return (
            kv_slots.at[t, :, pl.ds(pl.multiple_of(i * 2 * SLOTS, 16), 2 * SLOTS), :],
            home_ref.at[1:3, pl.ds(pl.multiple_of(seat * CHUNK + t * 2 * SLOTS, 16), 2 * SLOTS), :],
        )

    def key_tile(t, _):
        key, value = tile_rows(0, t), tile_rows(2, t)
        key_grad = jnp.zeros((TILE, HD), jnp.float32)
        value_grad = jnp.zeros((TILE, HD), jnp.float32)
        for cols in chunks:
            query, grad = head_rows(1, t, cols), head_rows(3, t, cols)
            scores = lax.dot_general(key, query, NT, preferred_element_type=jnp.float32)
            weights = jnp.exp2(scores * (SCALING * LOG2E) - stat_row(0, t, cols))
            dots = lax.dot_general(value, grad, NT, preferred_element_type=jnp.float32)
            dscore = weights * (dots - stat_row(1, t, cols))
            key_grad += jnp.dot(dscore.astype(jnp.bfloat16), query, preferred_element_type=jnp.float32)
            value_grad += jnp.dot(weights.astype(jnp.bfloat16), grad, preferred_element_type=jnp.float32)
        grads, term = norm_grads(raw[0, local_rows(t), :], gain_k_ref[...], key_grad * SCALING)
        terms[8:16, :] += term
        tile_codes = []
        for j in range(2):
            code = unit_codes(2 * t + j)
            tile_codes.append((code >> 3) * (2 * SLOTS) + j * SLOTS + (code & 7))
        spread = one_hot(tile_iota == jnp.concatenate(tile_codes, axis=1))
        for i, result in enumerate((grads, value_grad)):
            result = jnp.dot(spread, result.astype(jnp.bfloat16), preferred_element_type=jnp.float32)
            kv_slots[t, i] = result.astype(jnp.bfloat16)

        def start(n, _):
            i = (n + s) & (SEQ - 1)
            src, dst = kv_home(t, i)

            @pl.when(jnp.logical_not(to_self(i)))
            def _():
                remote(src, dst, home_send.at[1], home_recv.at[1], source(i)).start()

            return 0

        lax.fori_loop(0, SEQ, start, 0)

        @pl.when(same)
        def _():
            src, dst = kv_home(t, s)
            pltpu.make_async_copy(src, dst, home_recv.at[1]).start()

        return 0

    lax.fori_loop(0, TILES, key_tile, 0)


    def part_start(i, _):
        @pl.when(jnp.logical_not(to_self(i)))
        def _():
            remote(terms, parts.at[seat], part_sem.at[0], part_sem.at[1], source(i)).start()

        return 0

    lax.fori_loop(0, SEQ, part_start, 0)

    @pl.when(same)
    def _():
        pltpu.make_async_copy(terms, parts.at[seat], part_sem.at[1]).start()

    remote(parts, parts, part_sem.at[0], part_sem.at[1], sibling).wait_recv()
    partial[...] = jnp.sum(parts[...], axis=0)

    def cross_copy(i, dst):
        return remote(partial, cross.at[dst], cross_send.at[i], cross_recv.at[dst], (i >> 2, s, i & 3))

    def cross_start(i, _):
        @pl.when(i != corner)
        def _():
            cross_copy(i, corner).start()

        return 0

    def cross_finish(i, _):
        @pl.when(i != corner)
        def _():
            cross_copy(i, i).wait_recv()
            cross_copy(i, corner).wait_send()

        return 0

    cross[pl.ds(corner, 1)] = partial[...][None]
    lax.fori_loop(0, 8, cross_start, 0)
    lax.fori_loop(0, 8, cross_finish, 0)
    total_ref[...] = jnp.sum(cross[...], axis=0)


    @pl.when(same)
    def _():
        most = SEQ - 1
        for a in range(4):
            rows = slots.at[a, 0 : most * CHUNK, :]
            remote(rows, rows, route_send.at[a], route_recv.at[a], sibling).wait_send()
        rows = q_slots.at[0 : most * CHUNK, :]
        remote(rows, rows, home_send.at[0], home_recv.at[0], sibling).wait_send()
        rows = kv_slots.at[:, :, 0 : most * 2 * SLOTS, :]
        remote(rows, rows, home_send.at[1], home_recv.at[1], sibling).wait_send()
        rows = parts.at[0:most]
        remote(rows, rows, part_sem.at[0], part_sem.at[1], sibling).wait_send()

    @pl.when(jnp.logical_not(same))
    def _():
        for a in range(4):
            remote(slots.at[a], slots.at[a], route_send.at[a], route_recv.at[a], sibling).wait_send()
        remote(q_slots, q_slots, home_send.at[0], home_recv.at[0], sibling).wait_send()
        remote(kv_slots, kv_slots, home_send.at[1], home_recv.at[1], sibling).wait_send()
        remote(parts, parts, part_sem.at[0], part_sem.at[1], sibling).wait_send()

    for a in range(4):
        gather_sent(a)
    remote(q_slots, home_ref.at[0], home_send.at[0], home_recv.at[0], sibling).wait_recv()
    remote(home_ref.at[1:3], home_ref.at[1:3], home_send.at[1], home_recv.at[1], sibling).wait_recv()


def core(listing, k, q, v, g, gain_q, gain_k):
    bf16, f32 = jnp.bfloat16, jnp.float32
    dma = pltpu.SemaphoreType.DMA
    paths = len(PATHS)
    in_vmem = pl.BlockSpec(memory_space=pltpu.VMEM)
    return pl.pallas_call(
        core_kernel,
        name="core",
        in_specs=[in_vmem] * 7,
        out_specs=[pl.BlockSpec(memory_space=pl.ANY), in_vmem, in_vmem],
        out_shape=(
            jax.ShapeDtypeStruct((3, FLAT, HD), bf16),
            jax.ShapeDtypeStruct((SPAN, SPAN), bf16),
            jax.ShapeDtypeStruct((16, HD), f32),
        ),
        scratch_shapes=[
            pltpu.VMEM((4, FLAT, HD), bf16),
            pltpu.VMEM((4, FLAT, HD), bf16),
            pltpu.VMEM((SEQ, SHARE), jnp.int32),
            pltpu.VMEM((SEQ, SHARE), jnp.int32),
            pltpu.VMEM((SEQ, SHARE), jnp.int32),
            pltpu.VMEM((ROWS, FLAT), bf16),
            pltpu.VMEM((4, MEMBERS * ROWS, HD), bf16),
            pltpu.VMEM((2, ROWS, HD), bf16),
            pltpu.VMEM((ROWS, KEPT), f32),
            pltpu.VMEM((TILE, KEPT), f32),
            pltpu.VMEM((ROWS, 128), f32),
            pltpu.VMEM((ROWS, HD), bf16),
            pltpu.VMEM((FLAT, HD), bf16),
            pltpu.VMEM((TILES, 2, 2 * SLOTS * SEQ, HD), bf16),
            pltpu.VMEM((MEMBERS, 2, 8, SHARE), f32),
            pltpu.VMEM((2, MEMBERS * UNITS, SHARE), f32),
            pltpu.VMEM((16, HD), f32),
            pltpu.VMEM((SEQ, 16, HD), f32),
            pltpu.VMEM((16, HD), f32),
            pltpu.VMEM((8, 16, HD), f32),
            dma((2,)),
            dma((4,)),
            dma((4,)),
            dma((4,)),
            dma((4,)),
            dma((4, paths, 2)),
            dma((4, paths)),
            dma((4, paths)),
            dma((4, paths)),
            dma((4, paths)),
            dma((MEMBERS,)),
            dma((MEMBERS,)),
            dma((2,)),
            dma((2,)),
            dma((2,)),
            dma((8,)),
            dma((8,)),
        ],
        compiler_params=pltpu.CompilerParams(
            collective_id=0, has_side_effects=True, vmem_limit_bytes=VMEM_LIMIT
        ),
    )(listing, k, q, v, g, gain_q, gain_k)


def rows_kernel(back_ref, slots_ref, total_ref, q_ref, k_ref, v_ref, gain_q_ref, gain_k_ref):
    for i, ref in enumerate((q_ref, k_ref, v_ref)):
        for h in range(slots_ref.shape[1] // SPAN):
            rows = slots_ref[i, h * SPAN : (h + 1) * SPAN, :]
            rows = jnp.dot(back_ref[...], rows, preferred_element_type=jnp.float32)
            ref[0, :, h * HD : (h + 1) * HD] = rows.astype(jnp.bfloat16)
    gain_q_ref[...] = jnp.sum(total_ref[0:8, :], axis=0, keepdims=True)
    gain_k_ref[...] = jnp.sum(total_ref[8:16, :], axis=0, keepdims=True)


def to_rows(back, slots, total):
    width = HEAD_PART * HD
    parts = 2
    big = jax.ShapeDtypeStruct((1, SPAN, width), jnp.bfloat16)
    small = jax.ShapeDtypeStruct((1, HD), jnp.float32)
    return pl.pallas_call(
        rows_kernel,
        name="to_rows",
        grid=(parts,),
        in_specs=[
            pl.BlockSpec((SPAN, SPAN), lambda h: (0, 0)),
            pl.BlockSpec((3, FLAT // parts, HD), lambda h: (0, h, 0)),
            pl.BlockSpec((16, HD), lambda h: (0, 0)),
        ],
        out_specs=[pl.BlockSpec((1, SPAN, width // parts), lambda h: (0, 0, h))] * 3
        + [pl.BlockSpec((1, HD), lambda h: (0, 0))] * 2,
        out_shape=(big, big, big, small, small),
        compiler_params=pltpu.CompilerParams(vmem_limit_bytes=VMEM_LIMIT),
        cost_estimate=pl.CostEstimate(flops=3 * 10**8, bytes_accessed=3 * 10**6, transcendentals=0),
    )(back, slots, total)


def on_device(q_raw, k_raw, v_raw, out_grad, gain_q, gain_k, keep_list):
    home, back, total = core(
        keep_list.reshape(SEQ, SHARE),
        k_raw[0],
        q_raw[0],
        v_raw[0],
        out_grad[0],
        gain_q.reshape(1, HD),
        gain_k.reshape(1, HD),
    )
    q_out, k_out, v_out, gain_q_grad, gain_k_grad = to_rows(back, home, total)
    return q_out, k_out, v_out, gain_q_grad.reshape(HD), gain_k_grad.reshape(HD)


def solution(mesh):
    big = P("dp", "seq", "tensor")
    return jax.shard_map(
        on_device,
        mesh=mesh,
        in_specs=(big, big, big, big, P(), P(), P("dp", None)),
        out_specs=(big, big, big, P(), P()),
        check_vma=False,
    )
```

time: 154 us -> 133 us (0.86)
  Pallas kernels: 149 us -> 132 us
  other arithmetic: 3.49 us -> 0 us
    pallas_call x2, Pallas kernels: 149 us -> 132 us  [the longest x1 129 us: core(): pl.pallas_call(core_kernel, name='core', in_specs=[in_vmem] * 7, out_spec...]
where the time goes in v2:
time: 133 us; the launch traced here: 132 us
  Pallas kernels  132 us (99%)
    pallas_call x1, Pallas kernels, core(): pl.pallas_call(core_kernel, name='core', in_specs=[in_vmem] * 7, out_spec...  129 us
    pallas_call x1, Pallas kernels, to_rows(): pl.pallas_call(rows_kernel, name='to_rows', grid=(parts,), in_specs=[pl.B...  2.8 us

profile of v2, /device:TPU:1, one launch (start us, length us, event | category | flops | bytes accessed | tf_op | source)
XLA Modules:
  0.0 132.4 jit_solution(16161869082543726459)
XLA Ops:
  0.6 128.9 %core.1 = (bf16[3,1536,128]{2,1,0:T(8,128)(2,1)}, bf16[256,256]{1,0:T(8,128)(2,1)}, f32[16,128]{1,0:T(8,128)}) custom-call(s32[32,128]{1,0:T(8,128)} %bitcast.13, bf16[256,768]{1,0:T(8,128)(2,1)} %bitcast.9, bf16[256,768]{1,0:T(8,128)(2,1)} %bitcast.10, bf16[256,768]{1,0:T(8,128)(2,1)} %bitcast.11, bf16[256,768]{1,0:T(8,128)(2,1)} %bitcast.12, ...), custom_call_target="tpu_custom_call" | custom-call | tf_op jit(solution)/shard_map/core/pallas_call | solution.py:703
  129.6 2.8 %to_rows.1 = (bf16[1,256,768]{2,1,0:T(8,128)(2,1)}, bf16[1,256,768]{2,1,0:T(8,128)(2,1)}, bf16[1,256,768]{2,1,0:T(8,128)(2,1)}, f32[1,128]{1,0:T(1,128)}, f32[1,128]{1,0:T(1,128)}) custom-call(bf16[256,256]{1,0:T(8,128)(2,1)} %get-tuple-element.13.back_ref, bf16[3,1536,128]{2,1,0:T(8,128)(2,1)} %get-tuple-element.14.slots_ref, ...), custom_call_target="tpu_custom_call" | custom-call | flops 300000000 | bytes 3000000 | tf_op jit(solution)/shard_map/to_rows/pallas_call | solution.py:773

commit v3 on v2

v3 whole, which is shorter than its diff:
```python
import math

import jax
import jax.numpy as jnp
from jax import lax
from jax.experimental import pallas as pl
from jax.experimental.pallas import tpu as pltpu
from jax.sharding import PartitionSpec as P

MESH = pl.DeviceIdType.MESH
HD = 128
EPSILON = 1e-06
SEQ = 32
SPAN = 256
SHARE = 128
SLOTS = 8
HEAD_PART = 6
UNITS = 8
ROWS = UNITS * SHARE
CHUNK = UNITS * SLOTS
MEMBERS = 4
TARGETS = HEAD_PART * MEMBERS
OUT = TARGETS * CHUNK
FLAT = SEQ * CHUNK
KEPT = SEQ * SHARE
TILE = 256
TILES = ROWS // TILE
SCALING = 1.0 / math.sqrt(HD)
LOG2E = 1.4426950408889634
VMEM_LIMIT = 56 * 1024 * 1024

NT = (((1,), (1,)), ((), ()))

def place(x, clip, i):
    head, quarter = i >> 2, i & 3
    third = (head * 11) >> 5
    pair = head - 3 * third
    y = 2 * (x & 1) + (pair & 1)
    z = 4 * clip + 2 * third + (pair >> 1)
    return quarter & 1, y * 8 + z, (x & 2) + (quarter >> 1)


def my_place(dp, s, x):
    y, z = s >> 3, s & 7
    third, pair = (z >> 1) & 1, (y & 1) + 2 * (z & 1)
    return (x & 2) + (y >> 1), z >> 2, (3 * third + pair) * 4 + 2 * (x & 1) + dp, pair < 3


def one_hot(hit):
    return jnp.where(hit, 1.0, 0.0).astype(jnp.bfloat16)


def inverse_norm(x):
    return lax.rsqrt(jnp.mean(x * x, axis=-1, keepdims=True) + EPSILON)


def norm_grads(raw, gain, upstream):
    raw = raw.astype(jnp.float32)
    inverse = inverse_norm(raw)
    scaled = upstream * gain
    inner = jnp.mean(scaled * raw, axis=-1, keepdims=True)
    grads = inverse * scaled - raw * (inverse * inverse * inverse * inner)
    terms = upstream * raw * inverse
    return grads, jnp.sum(terms.reshape(-1, 8, HD), axis=0)


def lane_fold(x, fold):
    parts = [x[:, i * 128 : (i + 1) * 128] for i in range(x.shape[1] // 128)]
    total = parts[0]
    for part in parts[1:]:
        total = fold(total, part)
    return total


def core_kernel(
    list_ref,
    k_ref,
    q_ref,
    v_ref,
    g_ref,
    gain_q_ref,
    gain_k_ref,
    home_ref,
    back_ref,
    total_ref,
    slots,
    arrived,
    enc_ref,
    other,
    codes,
    pick,
    full,
    raw,
    scores_ref,
    dots_ref,
    sums,
    q_slots,
    kv_slots,
    stats,
    terms,
    part_bytes,
    parts,
    partial,
    cross,
    enc_sem,
    route_send,
    route_recv,
    near_send,
    near_recv,
    stat_send,
    stat_recv,
    home_send,
    home_recv,
    part_sem,
    cross_send,
    cross_recv,
):
    dp, s, x = lax.axis_index("dp"), lax.axis_index("seq"), lax.axis_index("tensor")
    head_x, clip, seat, active = my_place(dp, s, x)
    me = seat & 3
    sibling = (1 - dp, s, x)
    corner = dp * 4 + x
    same = active & (clip == dp) & (head_x == x)
    own_source = jnp.where(same, s, -1)
    own_target = jnp.where(same, seat, -1)

    def to_self(i):
        return i == own_source

    def target(i):
        return place(x, dp, i), i == own_target

    def source(i):
        return (clip, i, head_x)

    def member(i):
        return (i & 1, s, (x & 2) + (i >> 1))

    def remote(src, dst, send_sem, recv_sem, device):
        return pltpu.make_async_remote_copy(
            src_ref=src, dst_ref=dst, send_sem=send_sem, recv_sem=recv_sem, device_id=device, device_id_type=MESH
        )


    barrier = pltpu.get_barrier_semaphore()

    def greet_device(there):
        pl.semaphore_signal(barrier, inc=1, device_id=there, device_id_type=MESH)

    def greet_target(i, _):
        there, own = target(i)

        @pl.when(jnp.logical_not(own))
        def _():
            greet_device(there)

        return 0

    def greet_source(i, _):
        @pl.when(jnp.logical_not(to_self(i)))
        def _():
            greet_device(source(i))

        return 0

    def greet_corner(i, _):
        @pl.when(i != corner)
        def _():
            greet_device((i >> 2, s, i & 3))

        return 0

    @pl.when(active)
    def _():
        lax.fori_loop(0, SEQ, greet_source, 0)
        for step in (1, 2, 3):
            greet_device(member(me ^ step))

    lax.fori_loop(0, TARGETS, greet_target, 0)
    lax.fori_loop(0, 8, greet_corner, 0)


    listing = list_ref[...]
    from_block = listing >> 8
    hits = one_hot(jnp.concatenate([from_block == i for i in range(SEQ)], axis=0))
    earlier = lax.broadcasted_iota(jnp.int32, (SHARE, SHARE), 0) < lax.broadcasted_iota(jnp.int32, (SHARE, SHARE), 1)
    counts = jnp.dot(hits, one_hot(earlier), preferred_element_type=jnp.float32) * hits.astype(jnp.float32)
    rank = counts[0:SEQ]
    for i in range(1, SEQ):
        rank += counts[i * SEQ : (i + 1) * SEQ]
    rank = rank.astype(jnp.int32)
    enc_ref[...] = from_block * SLOTS + rank
    slot = lax.broadcasted_iota(jnp.int32, (SEQ, SHARE), 0) * SLOTS + rank
    slot = jnp.where(from_block == s, slot, -1)
    token = listing - s * SPAN

    def lanes(x, c):
        return jnp.concatenate([x[j : j + 1] for j in range(c * step // SHARE, (c + 1) * step // SHARE)], axis=1)

    step = 512
    iota = lax.broadcasted_iota(jnp.int32, (SPAN, step), 0)
    take = jnp.zeros((SPAN, SPAN), jnp.float32)
    back = jnp.zeros((SPAN, SPAN), jnp.float32)
    for c in range(KEPT // step):
        a = one_hot(iota == lanes(slot, c))
        b = one_hot(iota == lanes(token, c))
        take += lax.dot_general(a, b, NT, preferred_element_type=jnp.float32)
        back += lax.dot_general(b, a, NT, preferred_element_type=jnp.float32)
    take = take.astype(jnp.bfloat16)
    back_ref[...] = back.astype(jnp.bfloat16)

    def to_slots(i, ref):
        rows = jnp.dot(take, ref[...], preferred_element_type=jnp.float32).astype(jnp.bfloat16)
        for h in range(HEAD_PART):
            slots[i, h * SPAN : (h + 1) * SPAN, :] = rows[:, h * HD : (h + 1) * HD]

    def chunk(ref, a, i):
        return ref.at[a, pl.ds(pl.multiple_of(i * CHUNK, 16), CHUNK), :]

    turn = (3 * s) >> 2

    def route(a):
        def start(n, _):
            i = n + turn
            i = jnp.where(i < TARGETS, i, i - TARGETS)
            there, own = target(i)

            @pl.when(jnp.logical_not(own))
            def _():
                remote(chunk(slots, a, i), chunk(arrived, a, s), route_send.at[a], route_recv.at[a], there).start()

            return 0

        lax.fori_loop(0, TARGETS, start, 0)

        @pl.when(same)
        def _():
            pltpu.make_async_copy(chunk(slots, a, seat), chunk(arrived, a, s), route_recv.at[a]).start()

    to_slots(0, k_ref)
    arrivals = jnp.where(active, SEQ + 3, 0) - jnp.where(same, 2, 0)
    pl.semaphore_wait(barrier, TARGETS + 7 + arrivals)
    exchange = remote(enc_ref, other, enc_sem.at[0], enc_sem.at[1], sibling)

    @pl.when(active)
    def _():
        exchange.start()

    route(0)
    to_slots(1, q_ref)
    route(1)
    to_slots(2, v_ref)
    to_slots(3, g_ref)


    def unit_codes(u):
        return codes[pl.ds(UNITS * me + u, 1), :]

    def build_pick():
        exchange.wait()
        codes[...] = jnp.where(clip == dp, enc_ref[...], other[...])
        wide_iota = lax.broadcasted_iota(jnp.int32, (SHARE, 128), 1).astype(jnp.float32)
        for u in range(UNITS):
            code = unit_codes(u)
            code = (code >> 3) * CHUNK + u * SLOTS + (code & 7)
            wide = jnp.broadcast_to(code.astype(jnp.float32), (SHARE, 128)).T
            for c in range(FLAT // 128):
                pick[u * SHARE : (u + 1) * SHARE, c * 128 : (c + 1) * 128] = one_hot(wide == wide_iota + c * 128.0)

    own_rows = pl.ds(pl.multiple_of(me * ROWS, 256), ROWS)

    def to_dense(a):
        remote(arrived.at[a], arrived.at[a], route_send.at[a], route_recv.at[a], sibling).wait_recv()
        rows = jnp.dot(pick[...], arrived[a], preferred_element_type=jnp.float32)
        if a < 2:
            raw[a] = rows.astype(jnp.bfloat16)
            gain = (gain_k_ref, gain_q_ref)[a][...]
            rows = rows * inverse_norm(rows) * gain
        full[a, own_rows, :] = rows.astype(jnp.bfloat16)


    def rows_of(a, i):
        return full.at[a, pl.ds(pl.multiple_of(i * ROWS, ROWS), ROWS), :]

    def near(a, way, rows, there):
        return remote(rows_of(a, rows), rows_of(a, rows), near_send.at[a, way], near_recv.at[a, way], member(there))

    def gather_start(a):
        near(a, 0, me, me ^ 2).start()
        near(a, 1, me, me ^ 1).start()

    def gather_pass(a):
        near(a, 0, me ^ 2, me).wait_recv()
        near(a, 2, me ^ 2, me ^ 1).start()

    def gather_finish(a):
        near(a, 1, me ^ 1, me).wait_recv()
        near(a, 2, me ^ 3, me).wait_recv()

    def gather_sent(a):
        near(a, 0, me, me ^ 2).wait_send()
        near(a, 1, me, me ^ 1).wait_send()
        near(a, 2, me ^ 2, me ^ 1).wait_send()


    chunks = [slice(i * step, (i + 1) * step) for i in range(KEPT // step)]

    def head_rows(a, cols):
        return full[a, cols, :]

    def tile_rows(a, t):
        return full[a, pl.ds(pl.multiple_of(me * ROWS + t * TILE, TILE), TILE), :]

    def local_rows(t):
        return pl.ds(pl.multiple_of(t * TILE, TILE), TILE)

    def store_stat(i, t, value):
        wide = jnp.broadcast_to(value, (TILE, 128)).T
        for j in range(TILE // SHARE):
            stats[me, i, pl.ds(2 * t + j, 1), :] = wide[0:1, j * SHARE : (j + 1) * SHARE]

    def score_tile(t, _):
        query = tile_rows(1, t)
        rows = local_rows(t)
        top = None
        for cols in chunks:
            scores = lax.dot_general(query, head_rows(0, cols), NT, preferred_element_type=jnp.float32)
            scores = scores * (SCALING * LOG2E)
            scores_ref[rows, cols] = scores
            part = lane_fold(scores, jnp.maximum)
            top = part if top is None else jnp.maximum(top, part)
        top = jnp.max(top, axis=-1, keepdims=True)
        total = jnp.zeros((TILE, 128), jnp.float32)
        for cols in chunks:
            weights = jnp.exp2(scores_ref[rows, cols] - top)
            scores_ref[rows, cols] = weights
            total += lane_fold(weights, jnp.add)
        total = jnp.sum(total, axis=-1, keepdims=True)
        sums[rows, :] = jnp.broadcast_to(total, (TILE, 128))
        store_stat(0, t, top + jnp.log2(total))

        @pl.when(t == 1)
        def _():
            to_dense(2)
            gather_start(2)
            gather_start(1)

        return 0

    def spread_tile(t, rows):
        tile_iota = lax.broadcasted_iota(jnp.int32, (2 * SLOTS * SEQ, TILE), 0)
        tile_codes = []
        for j in range(2):
            code = unit_codes(2 * t + j)
            tile_codes.append((code >> 3) * (2 * SLOTS) + j * SLOTS + (code & 7))
        spread = one_hot(tile_iota == jnp.concatenate(tile_codes, axis=1))
        rows = jnp.dot(spread, rows.astype(jnp.bfloat16), preferred_element_type=jnp.float32)
        return rows.astype(jnp.bfloat16).reshape(SEQ, 2 * SLOTS, HD)

    def query_tile(t, _):
        grad = tile_rows(3, t)
        rows = local_rows(t)
        weighted = jnp.zeros((TILE, 128), jnp.float32)
        for cols in chunks:
            dots = lax.dot_general(grad, head_rows(2, cols), NT, preferred_element_type=jnp.float32)
            dots_ref[:, cols] = dots
            weighted += lane_fold(scores_ref[rows, cols] * dots, jnp.add)
        share = 1.0 / sums[rows, 0:1]
        delta = jnp.sum(weighted, axis=-1, keepdims=True) * share
        result = jnp.zeros((TILE, HD), jnp.float32)
        for cols in chunks:
            dscore = (scores_ref[rows, cols] * share) * (dots_ref[:, cols] - delta)
            result += jnp.dot(dscore.astype(jnp.bfloat16), head_rows(0, cols), preferred_element_type=jnp.float32)
        grads, term = norm_grads(raw[1, rows, :], gain_q_ref[...], result * SCALING)
        terms[0:8, :] += term
        store_stat(1, t, delta)

        q_slots[:, pl.ds(pl.multiple_of(t * 2 * SLOTS, 16), 2 * SLOTS), :] = spread_tile(t, grads)

        @pl.when(t == 0)
        def _():
            gather_pass(1)

        @pl.when(t == 1)
        def _():
            gather_pass(3)

        return 0


    def stat_copy(rows, there):
        return remote(stats.at[rows], stats.at[rows], stat_send.at[there], stat_recv.at[rows], member(there))

    def stat_start():
        for step in (1, 2, 3):
            stat_copy(me, me ^ step).start()

    def stat_finish():
        for step in (1, 2, 3):
            stat_copy(me ^ step, me ^ step).wait_recv()
            stat_copy(me, me ^ step).wait_send()


    def q_home(i):
        return q_slots.at[i], home_ref.at[0, pl.ds(pl.multiple_of(seat * CHUNK, CHUNK), CHUNK), :]

    def kv_home(half, i):
        count = CHUNK // 2
        return (
            kv_slots.at[:, i, pl.ds(pl.multiple_of(half * count, count), count), :],
            home_ref.at[1:3, pl.ds(pl.multiple_of(seat * CHUNK + half * count, count), count), :],
        )

    def send_home(copies, sem):
        def start(n, _):
            i = (n + s) & (SEQ - 1)
            src, dst = copies(i)

            @pl.when(jnp.logical_not(to_self(i)))
            def _():
                remote(src, dst, home_send.at[sem], home_recv.at[sem], source(i)).start()

            return 0

        lax.fori_loop(0, SEQ, start, 0)

        @pl.when(same)
        def _():
            src, dst = copies(s)
            pltpu.make_async_copy(src, dst, home_recv.at[sem]).start()


    def stat_row(i, cols):
        units = range(cols.start // SHARE, cols.stop // SHARE)
        return jnp.concatenate([stats[u // UNITS, i, u % UNITS : u % UNITS + 1, :] for u in units], axis=1)

    def key_tile(t, _):
        key, value = tile_rows(0, t), tile_rows(2, t)
        key_grad = jnp.zeros((TILE, HD), jnp.float32)
        value_grad = jnp.zeros((TILE, HD), jnp.float32)
        for cols in chunks:
            query, grad = head_rows(1, cols), head_rows(3, cols)
            scores = lax.dot_general(key, query, NT, preferred_element_type=jnp.float32)
            weights = jnp.exp2(scores * (SCALING * LOG2E) - stat_row(0, cols))
            dots = lax.dot_general(value, grad, NT, preferred_element_type=jnp.float32)
            dscore = weights * (dots - stat_row(1, cols))
            key_grad += jnp.dot(dscore.astype(jnp.bfloat16), query, preferred_element_type=jnp.float32)
            value_grad += jnp.dot(weights.astype(jnp.bfloat16), grad, preferred_element_type=jnp.float32)
        grads, term = norm_grads(raw[0, local_rows(t), :], gain_k_ref[...], key_grad * SCALING)
        terms[8:16, :] += term
        for i, result in enumerate((grads, value_grad)):
            kv_slots[i, :, pl.ds(pl.multiple_of(t * 2 * SLOTS, 16), 2 * SLOTS), :] = spread_tile(t, result)

        @pl.when((t & 1) == 1)
        def _():
            send_home(lambda i: kv_home(t >> 1, i), 1)

        return 0


    def part_start(i, _):
        @pl.when(jnp.logical_not(to_self(i)))
        def _():
            remote(terms, parts.at[seat], part_sem.at[0], part_sem.at[1], source(i)).start()

        return 0

    @pl.when(active)
    def _():
        build_pick()
        to_dense(0)
        gather_start(0)

    route(2)

    @pl.when(active)
    def _():
        to_dense(1)
        gather_pass(0)

    route(3)

    @pl.when(active)
    def _():
        terms[...] = jnp.zeros_like(terms)
        gather_finish(0)
        lax.fori_loop(0, TILES, score_tile, 0)
        gather_pass(2)
        to_dense(3)
        gather_start(3)
        gather_finish(2)
        lax.fori_loop(0, TILES, query_tile, 0)
        stat_start()
        send_home(q_home, 0)
        gather_finish(1)
        gather_finish(3)
        stat_finish()
        lax.fori_loop(0, TILES, key_tile, 0)
        lax.fori_loop(0, SEQ, part_start, 0)

        @pl.when(same)
        def _():
            pltpu.make_async_copy(terms, parts.at[seat], part_sem.at[1]).start()

    remote(parts, parts, part_sem.at[0], part_sem.at[1], sibling).wait_recv()
    partial[...] = jnp.sum(parts[...], axis=0)

    def cross_copy(i, dst):
        return remote(partial, cross.at[dst], cross_send.at[i], cross_recv.at[dst], (i >> 2, s, i & 3))

    def cross_start(i, _):
        @pl.when(i != corner)
        def _():
            cross_copy(i, corner).start()

        return 0

    def cross_finish(i, _):
        @pl.when(i != corner)
        def _():
            cross_copy(i, i).wait_recv()
            cross_copy(i, corner).wait_send()

        return 0

    cross[pl.ds(corner, 1)] = partial[...][None]
    lax.fori_loop(0, 8, cross_start, 0)
    lax.fori_loop(0, 8, cross_finish, 0)
    total_ref[...] = jnp.sum(cross[...], axis=0)


    def sent(targets, sources):
        for a in range(4):
            rows = slots.at[a, 0 : targets * CHUNK, :]
            remote(rows, rows, route_send.at[a], route_recv.at[a], sibling).wait_send()
        if sources:
            for a in range(4):
                gather_sent(a)
            rows = q_slots.at[0:sources]
            remote(rows, rows, home_send.at[0], home_recv.at[0], sibling).wait_send()
            rows = kv_slots.at[:, 0:sources]
            remote(rows, rows, home_send.at[1], home_recv.at[1], sibling).wait_send()
            rows = part_bytes.at[0:sources]
            remote(rows, rows, part_sem.at[0], part_sem.at[1], sibling).wait_send()

    @pl.when(same)
    def _():
        sent(TARGETS - 1, SEQ - 1)

    @pl.when(active & jnp.logical_not(same))
    def _():
        sent(TARGETS, SEQ)

    @pl.when(jnp.logical_not(active))
    def _():
        sent(TARGETS, 0)

    remote(home_ref.at[0], home_ref.at[0], home_send.at[0], home_recv.at[0], sibling).wait_recv()
    remote(home_ref.at[1:3], home_ref.at[1:3], home_send.at[1], home_recv.at[1], sibling).wait_recv()


def core(listing, k, q, v, g, gain_q, gain_k):
    bf16, f32 = jnp.bfloat16, jnp.float32
    dma = pltpu.SemaphoreType.DMA
    in_vmem = pl.BlockSpec(memory_space=pltpu.VMEM)
    return pl.pallas_call(
        core_kernel,
        name="core",
        in_specs=[in_vmem] * 7,
        out_specs=[pl.BlockSpec(memory_space=pl.ANY), in_vmem, in_vmem],
        out_shape=(
            jax.ShapeDtypeStruct((3, OUT, HD), bf16),
            jax.ShapeDtypeStruct((SPAN, SPAN), bf16),
            jax.ShapeDtypeStruct((16, HD), f32),
        ),
        scratch_shapes=[
            pltpu.VMEM((4, OUT, HD), bf16),
            pltpu.VMEM((4, FLAT, HD), bf16),
            pltpu.VMEM((SEQ, SHARE), jnp.int32),
            pltpu.VMEM((SEQ, SHARE), jnp.int32),
            pltpu.VMEM((SEQ, SHARE), jnp.int32),
            pltpu.VMEM((ROWS, FLAT), bf16),
            pltpu.VMEM((4, KEPT, HD), bf16),
            pltpu.VMEM((2, ROWS, HD), bf16),
            pltpu.VMEM((ROWS, KEPT), f32),
            pltpu.VMEM((TILE, KEPT), f32),
            pltpu.VMEM((ROWS, 128), f32),
            pltpu.VMEM((SEQ, CHUNK, HD), bf16),
            pltpu.VMEM((2, SEQ, CHUNK, HD), bf16),
            pltpu.VMEM((MEMBERS, 2, 8, SHARE), f32),
            pltpu.VMEM((16, HD), f32),
            pltpu.VMEM((SEQ, 16, HD), f32),
            pltpu.VMEM((TARGETS, 16, HD), f32),
            pltpu.VMEM((16, HD), f32),
            pltpu.VMEM((8, 16, HD), f32),
            dma((2,)),
            dma((4,)),
            dma((4,)),
            dma((4, 3)),
            dma((4, 3)),
            dma((MEMBERS,)),
            dma((MEMBERS,)),
            dma((2,)),
            dma((2,)),
            dma((2,)),
            dma((8,)),
            dma((8,)),
        ],
        compiler_params=pltpu.CompilerParams(
            collective_id=0, has_side_effects=True, vmem_limit_bytes=VMEM_LIMIT
        ),
    )(listing, k, q, v, g, gain_q, gain_k)


def rows_kernel(back_ref, slots_ref, total_ref, q_ref, k_ref, v_ref, gain_q_ref, gain_k_ref):
    for i, ref in enumerate((q_ref, k_ref, v_ref)):
        for h in range(slots_ref.shape[1] // SPAN):
            rows = slots_ref[i, h * SPAN : (h + 1) * SPAN, :]
            rows = jnp.dot(back_ref[...], rows, preferred_element_type=jnp.float32)
            ref[0, :, h * HD : (h + 1) * HD] = rows.astype(jnp.bfloat16)
    gain_q_ref[...] = jnp.sum(total_ref[0:8, :], axis=0, keepdims=True)
    gain_k_ref[...] = jnp.sum(total_ref[8:16, :], axis=0, keepdims=True)


def to_rows(back, slots, total):
    width = HEAD_PART * HD
    parts = 2
    big = jax.ShapeDtypeStruct((1, SPAN, width), jnp.bfloat16)
    small = jax.ShapeDtypeStruct((1, HD), jnp.float32)
    return pl.pallas_call(
        rows_kernel,
        name="to_rows",
        grid=(parts,),
        in_specs=[
            pl.BlockSpec((SPAN, SPAN), lambda h: (0, 0)),
            pl.BlockSpec((3, OUT // parts, HD), lambda h: (0, h, 0)),
            pl.BlockSpec((16, HD), lambda h: (0, 0)),
        ],
        out_specs=[pl.BlockSpec((1, SPAN, width // parts), lambda h: (0, 0, h))] * 3
        + [pl.BlockSpec((1, HD), lambda h: (0, 0))] * 2,
        out_shape=(big, big, big, small, small),
        compiler_params=pltpu.CompilerParams(vmem_limit_bytes=VMEM_LIMIT),
        cost_estimate=pl.CostEstimate(flops=3 * 10**8, bytes_accessed=3 * 10**6, transcendentals=0),
    )(back, slots, total)


def on_device(q_raw, k_raw, v_raw, out_grad, gain_q, gain_k, keep_list):
    home, back, total = core(
        keep_list.reshape(SEQ, SHARE),
        k_raw[0],
        q_raw[0],
        v_raw[0],
        out_grad[0],
        gain_q.reshape(1, HD),
        gain_k.reshape(1, HD),
    )
    q_out, k_out, v_out, gain_q_grad, gain_k_grad = to_rows(back, home, total)
    return q_out, k_out, v_out, gain_q_grad.reshape(HD), gain_k_grad.reshape(HD)


def solution(mesh):
    big = P("dp", "seq", "tensor")
    return jax.shard_map(
        on_device,
        mesh=mesh,
        in_specs=(big, big, big, big, P(), P(), P("dp", None)),
        out_specs=(big, big, big, P(), P()),
        check_vma=False,
    )
```

time: 133 us -> 128 us (0.962)
  Pallas kernels: 132 us -> 127 us
    pallas_call x1, Pallas kernels: 129 us -> 124 us  [core(): pl.pallas_call(core_kernel, name='core', in_specs=[in_vmem] * 7, out_spec...]
where the time goes in v3:
time: 128 us
  Pallas kernels  127 us (99%)
    pallas_call x1, Pallas kernels, core(): pl.pallas_call(core_kernel, name='core', in_specs=[in_vmem] * 7, out_spec...  124 us
    pallas_call x1, Pallas kernels, to_rows(): pl.pallas_call(rows_kernel, name='to_rows', grid=(parts,), in_specs=[pl.B...  2.8 us

profile of v3, /device:TPU:1, one launch (start us, length us, event | category | flops | bytes accessed | tf_op | source)
XLA Modules:
  0.0 127.8 jit_solution(3517659805473487206)
XLA Ops:
  0.6 124.3 %core.1 = (bf16[3,1536,128]{2,1,0:T(8,128)(2,1)}, bf16[256,256]{1,0:T(8,128)(2,1)}, f32[16,128]{1,0:T(8,128)}) custom-call(s32[32,128]{1,0:T(8,128)} %bitcast.13, bf16[256,768]{1,0:T(8,128)(2,1)} %bitcast.9, bf16[256,768]{1,0:T(8,128)(2,1)} %bitcast.10, bf16[256,768]{1,0:T(8,128)(2,1)} %bitcast.11, bf16[256,768]{1,0:T(8,128)(2,1)} %bitcast.12, ...), custom_call_target="tpu_custom_call" | custom-call | tf_op jit(solution)/shard_map/core/pallas_call | solution.py:566
  125.0 2.8 %to_rows.1 = (bf16[1,256,768]{2,1,0:T(8,128)(2,1)}, bf16[1,256,768]{2,1,0:T(8,128)(2,1)}, bf16[1,256,768]{2,1,0:T(8,128)(2,1)}, f32[1,128]{1,0:T(1,128)}, f32[1,128]{1,0:T(1,128)}) custom-call(bf16[256,256]{1,0:T(8,128)(2,1)} %get-tuple-element.13.back_ref, bf16[3,1536,128]{2,1,0:T(8,128)(2,1)} %get-tuple-element.14.slots_ref, ...), custom_call_target="tpu_custom_call" | custom-call | flops 300000000 | bytes 3000000 | tf_op jit(solution)/shard_map/to_rows/pallas_call | solution.py:630

commit v4 on v3

--- a/solution.py
+++ b/solution.py
@@ -25,6 +25,7 @@
 KEPT = SEQ * SHARE
 TILE = 256
 TILES = ROWS // TILE
+PIECE = 128
 SCALING = 1.0 / math.sqrt(HD)
 LOG2E = 1.4426950408889634
 VMEM_LIMIT = 56 * 1024 * 1024
@@ -219,8 +220,16 @@
 
     turn = (3 * s) >> 2
 
-    def route(a):
+    def route(a, first, last, beside=None):
         def start(n, _):
+            if beside is not None:
+
+                @pl.when(n < first + ROWS // PIECE)
+                def _():
+                    @pl.when(active)
+                    def _():
+                        piece(beside, n - first).start()
+
             i = n + turn
             i = jnp.where(i < TARGETS, i, i - TARGETS)
             there, own = target(i)
@@ -231,11 +240,20 @@
 
             return 0
 
-        lax.fori_loop(0, TARGETS, start, 0)
-
-        @pl.when(same)
-        def _():
-            pltpu.make_async_copy(chunk(slots, a, seat), chunk(arrived, a, s), route_recv.at[a]).start()
+        lax.fori_loop(first, last, start, 0)
+
+        if last == TARGETS:
+
+            @pl.when(same)
+            def _():
+                pltpu.make_async_copy(chunk(slots, a, seat), chunk(arrived, a, s), route_recv.at[a]).start()
+
+    def rows_of(a, i):
+        return full.at[a, pl.ds(pl.multiple_of(i * ROWS, ROWS), ROWS), :]
+
+    def piece(a, n):
+        rows = full.at[a, pl.ds(pl.multiple_of(me * ROWS + n * PIECE, PIECE), PIECE), :]
+        return remote(rows, rows, near_send.at[a, 0], near_recv.at[a, 0], member(me ^ 2))
 
     to_slots(0, k_ref)
     arrivals = jnp.where(active, SEQ + 3, 0) - jnp.where(same, 2, 0)
@@ -246,9 +264,9 @@
     def _():
         exchange.start()
 
-    route(0)
+    route(0, 0, TARGETS)
     to_slots(1, q_ref)
-    route(1)
+    route(1, 0, TARGETS)
     to_slots(2, v_ref)
     to_slots(3, g_ref)
 
@@ -267,6 +285,30 @@
             for c in range(FLAT // 128):
                 pick[u * SHARE : (u + 1) * SHARE, c * 128 : (c + 1) * 128] = one_hot(wide == wide_iota + c * 128.0)
 
+
+    def near(a, way, rows, there):
+        return remote(rows_of(a, rows), rows_of(a, rows), near_send.at[a, way], near_recv.at[a, way], member(there))
+
+    def gather_rest():
+        def start(n, _):
+            piece(3, n).start()
+            return 0
+
+        lax.fori_loop(0, ROWS // PIECE, start, 0)
+
+    def gather_pass(a):
+        near(a, 0, me ^ 2, me).wait_recv()
+        near(a, 2, me ^ 2, me ^ 1).start()
+
+    def gather_finish(a):
+        near(a, 1, me ^ 1, me).wait_recv()
+        near(a, 2, me ^ 3, me).wait_recv()
+
+    def gather_sent(a):
+        near(a, 0, me, me ^ 2).wait_send()
+        near(a, 1, me, me ^ 1).wait_send()
+        near(a, 2, me ^ 2, me ^ 1).wait_send()
+
     own_rows = pl.ds(pl.multiple_of(me * ROWS, 256), ROWS)
 
     def to_dense(a):
@@ -277,30 +319,7 @@
             gain = (gain_k_ref, gain_q_ref)[a][...]
             rows = rows * inverse_norm(rows) * gain
         full[a, own_rows, :] = rows.astype(jnp.bfloat16)
-
-
-    def rows_of(a, i):
-        return full.at[a, pl.ds(pl.multiple_of(i * ROWS, ROWS), ROWS), :]
-
-    def near(a, way, rows, there):
-        return remote(rows_of(a, rows), rows_of(a, rows), near_send.at[a, way], near_recv.at[a, way], member(there))
-
-    def gather_start(a):
-        near(a, 0, me, me ^ 2).start()
         near(a, 1, me, me ^ 1).start()
-
-    def gather_pass(a):
-        near(a, 0, me ^ 2, me).wait_recv()
-        near(a, 2, me ^ 2, me ^ 1).start()
-
-    def gather_finish(a):
-        near(a, 1, me ^ 1, me).wait_recv()
-        near(a, 2, me ^ 3, me).wait_recv()
-
-    def gather_sent(a):
-        near(a, 0, me, me ^ 2).wait_send()
-        near(a, 1, me, me ^ 1).wait_send()
-        near(a, 2, me ^ 2, me ^ 1).wait_send()
 
 
     chunks = [slice(i * step, (i + 1) * step) for i in range(KEPT // step)]
@@ -339,12 +358,6 @@
         sums[rows, :] = jnp.broadcast_to(total, (TILE, 128))
         store_stat(0, t, top + jnp.log2(total))
 
-        @pl.when(t == 1)
-        def _():
-            to_dense(2)
-            gather_start(2)
-            gather_start(1)
-
         return 0
 
     def spread_tile(t, rows):
@@ -377,13 +390,9 @@
 
         q_slots[:, pl.ds(pl.multiple_of(t * 2 * SLOTS, 16), 2 * SLOTS), :] = spread_tile(t, grads)
 
-        @pl.when(t == 0)
-        def _():
-            gather_pass(1)
-
-        @pl.when(t == 1)
-        def _():
-            gather_pass(3)
+        @pl.when((t & 1) == 1)
+        def _():
+            send_home(lambda i: q_home(t >> 1, i), 0)
 
         return 0
 
@@ -401,8 +410,12 @@
             stat_copy(me, me ^ step).wait_send()
 
 
-    def q_home(i):
-        return q_slots.at[i], home_ref.at[0, pl.ds(pl.multiple_of(seat * CHUNK, CHUNK), CHUNK), :]
+    def q_home(half, i):
+        count = CHUNK // 2
+        return (
+            q_slots.at[i, pl.ds(pl.multiple_of(half * count, count), count), :],
+            home_ref.at[0, pl.ds(pl.multiple_of(seat * CHUNK + half * count, count), count), :],
+        )
 
     def kv_home(half, i):
         count = CHUNK // 2
@@ -469,29 +482,36 @@
     def _():
         build_pick()
         to_dense(0)
-        gather_start(0)
-
-    route(2)
+
+    route(2, 0, TARGETS, beside=0)
 
     @pl.when(active)
     def _():
         to_dense(1)
+
+    route(3, 0, TARGETS // 2, beside=1)
+
+    @pl.when(active)
+    def _():
+        terms[...] = jnp.zeros_like(terms)
         gather_pass(0)
-
-    route(3)
+        gather_finish(0)
+        lax.fori_loop(0, TILES // 2, score_tile, 0)
+        to_dense(2)
+
+    route(3, TARGETS // 2, TARGETS, beside=2)
 
     @pl.when(active)
     def _():
-        terms[...] = jnp.zeros_like(terms)
-        gather_finish(0)
-        lax.fori_loop(0, TILES, score_tile, 0)
+        gather_pass(1)
+        lax.fori_loop(TILES // 2, TILES, score_tile, 0)
         gather_pass(2)
         to_dense(3)
-        gather_start(3)
+        gather_rest()
         gather_finish(2)
         lax.fori_loop(0, TILES, query_tile, 0)
         stat_start()
-        send_home(q_home, 0)
+        gather_pass(3)
         gather_finish(1)
         gather_finish(3)
         stat_finish()

time: 128 us -> 129 us (level); the launches traced: 128 us -> 127 us
    pallas_call x1, Pallas kernels: 124 us -> 123 us  [core(): pl.pallas_call(core_kernel, name='core', in_specs=[in_vmem] * 7, out_spec...]
where the time goes in v4:
time: 129 us; the launch traced here: 127 us
  Pallas kernels  126 us (98%)
    pallas_call x1, Pallas kernels, core(): pl.pallas_call(core_kernel, name='core', in_specs=[in_vmem] * 7, out_spec...  123 us
    pallas_call x1, Pallas kernels, to_rows(): pl.pallas_call(rows_kernel, name='to_rows', grid=(parts,), in_specs=[pl.B...  2.8 us

profile of v4, /device:TPU:1, one launch (start us, length us, event | category | flops | bytes accessed | tf_op | source)
XLA Modules:
  0.0 126.5 jit_solution(4598169330410346824)
XLA Ops:
  0.6 123.0 %core.1 = (bf16[3,1536,128]{2,1,0:T(8,128)(2,1)}, bf16[256,256]{1,0:T(8,128)(2,1)}, f32[16,128]{1,0:T(8,128)}) custom-call(s32[32,128]{1,0:T(8,128)} %bitcast.13, bf16[256,768]{1,0:T(8,128)(2,1)} %bitcast.9, bf16[256,768]{1,0:T(8,128)(2,1)} %bitcast.10, bf16[256,768]{1,0:T(8,128)(2,1)} %bitcast.11, bf16[256,768]{1,0:T(8,128)(2,1)} %bitcast.12, ...), custom_call_target="tpu_custom_call" | custom-call | tf_op jit(solution)/shard_map/core/pallas_call | solution.py:586
  123.7 2.8 %to_rows.1 = (bf16[1,256,768]{2,1,0:T(8,128)(2,1)}, bf16[1,256,768]{2,1,0:T(8,128)(2,1)}, bf16[1,256,768]{2,1,0:T(8,128)(2,1)}, f32[1,128]{1,0:T(1,128)}, f32[1,128]{1,0:T(1,128)}) custom-call(bf16[256,256]{1,0:T(8,128)(2,1)} %get-tuple-element.13.back_ref, bf16[3,1536,128]{2,1,0:T(8,128)(2,1)} %get-tuple-element.14.slots_ref, ...), custom_call_target="tpu_custom_call" | custom-call | flops 300000000 | bytes 3000000 | tf_op jit(solution)/shard_map/to_rows/pallas_call | solution.py:650

commit v5 on v4

--- a/solution.py
+++ b/solution.py
@@ -32,19 +32,22 @@
 
 NT = (((1,), (1,)), ((), ()))
 
-def place(x, clip, i):
+def place(clip, i):
     head, quarter = i >> 2, i & 3
     third = (head * 11) >> 5
     pair = head - 3 * third
-    y = 2 * (x & 1) + (pair & 1)
-    z = 4 * clip + 2 * third + (pair >> 1)
-    return quarter & 1, y * 8 + z, (x & 2) + (quarter >> 1)
-
-
-def my_place(dp, s, x):
+    odd = pair >> 1
+    y = 2 * ((pair & 1) + odd * third) + (quarter >> 1)
+    z = 4 * clip + 2 * third + odd
+    return quarter & 1, y * 8 + z
+
+
+def my_place(dp, s):
     y, z = s >> 3, s & 7
-    third, pair = (z >> 1) & 1, (y & 1) + 2 * (z & 1)
-    return (x & 2) + (y >> 1), z >> 2, (3 * third + pair) * 4 + 2 * (x & 1) + dp, pair < 3
+    third, odd, high = (z >> 1) & 1, z & 1, y >> 1
+    pair = high + odd * (2 - high)
+    active = (odd == 0) | (high == third)
+    return z >> 2, (3 * third + pair) * 4 + 2 * (y & 1) + dp, active
 
 
 def one_hot(hit):
@@ -117,11 +120,11 @@
     cross_recv,
 ):
     dp, s, x = lax.axis_index("dp"), lax.axis_index("seq"), lax.axis_index("tensor")
-    head_x, clip, seat, active = my_place(dp, s, x)
+    clip, seat, active = my_place(dp, s)
     me = seat & 3
     sibling = (1 - dp, s, x)
     corner = dp * 4 + x
-    same = active & (clip == dp) & (head_x == x)
+    same = active & (clip == dp)
     own_source = jnp.where(same, s, -1)
     own_target = jnp.where(same, seat, -1)
 
@@ -129,13 +132,13 @@
         return i == own_source
 
     def target(i):
-        return place(x, dp, i), i == own_target
+        return place(dp, i) + (x,), i == own_target
 
     def source(i):
-        return (clip, i, head_x)
+        return (clip, i, x)
 
     def member(i):
-        return (i & 1, s, (x & 2) + (i >> 1))
+        return (i & 1, (s & 23) + 8 * (i >> 1), x)
 
     def remote(src, dst, send_sem, recv_sem, device):
         return pltpu.make_async_remote_copy(

time: 129 us -> 120 us (0.930); the launches traced: 127 us -> 120 us
  Pallas kernels: 126 us -> 120 us
    pallas_call x1, Pallas kernels: 123 us -> 117 us  [core(): pl.pallas_call(core_kernel, name='core', in_specs=[in_vmem] * 7, out_spec...]
where the time goes in v5:
time: 120 us
  Pallas kernels  120 us (100%)
    pallas_call x1, Pallas kernels, core(): pl.pallas_call(core_kernel, name='core', in_specs=[in_vmem] * 7, out_spec...  117 us
    pallas_call x1, Pallas kernels, to_rows(): pl.pallas_call(rows_kernel, name='to_rows', grid=(parts,), in_specs=[pl.B...  2.8 us

profile of v5, /device:TPU:1, one launch (start us, length us, event | category | flops | bytes accessed | tf_op | source)
XLA Modules:
  0.0 120.4 jit_solution(10842176393121743275)
XLA Ops:
  0.6 116.9 %core.1 = (bf16[3,1536,128]{2,1,0:T(8,128)(2,1)}, bf16[256,256]{1,0:T(8,128)(2,1)}, f32[16,128]{1,0:T(8,128)}) custom-call(s32[32,128]{1,0:T(8,128)} %bitcast.13, bf16[256,768]{1,0:T(8,128)(2,1)} %bitcast.9, bf16[256,768]{1,0:T(8,128)(2,1)} %bitcast.10, bf16[256,768]{1,0:T(8,128)(2,1)} %bitcast.11, bf16[256,768]{1,0:T(8,128)(2,1)} %bitcast.12, ...), custom_call_target="tpu_custom_call" | custom-call | tf_op jit(solution)/shard_map/core/pallas_call | solution.py:589
  117.5 2.8 %to_rows.1 = (bf16[1,256,768]{2,1,0:T(8,128)(2,1)}, bf16[1,256,768]{2,1,0:T(8,128)(2,1)}, bf16[1,256,768]{2,1,0:T(8,128)(2,1)}, f32[1,128]{1,0:T(1,128)}, f32[1,128]{1,0:T(1,128)}) custom-call(bf16[256,256]{1,0:T(8,128)(2,1)} %get-tuple-element.13.back_ref, bf16[3,1536,128]{2,1,0:T(8,128)(2,1)} %get-tuple-element.14.slots_ref, ...), custom_call_target="tpu_custom_call" | custom-call | flops 300000000 | bytes 3000000 | tf_op jit(solution)/shard_map/to_rows/pallas_call | solution.py:653

commit v6 on v5

--- a/solution.py
+++ b/solution.py
@@ -23,7 +23,8 @@
 OUT = TARGETS * CHUNK
 FLAT = SEQ * CHUNK
 KEPT = SEQ * SHARE
-TILE = 256
+TILE = 512
+PART = TILE // SHARE * SLOTS
 TILES = ROWS // TILE
 PIECE = 128
 SCALING = 1.0 / math.sqrt(HD)
@@ -194,24 +195,18 @@
         rank += counts[i * SEQ : (i + 1) * SEQ]
     rank = rank.astype(jnp.int32)
     enc_ref[...] = from_block * SLOTS + rank
-    slot = lax.broadcasted_iota(jnp.int32, (SEQ, SHARE), 0) * SLOTS + rank
-    slot = jnp.where(from_block == s, slot, -1)
+    slot = lax.broadcasted_iota(jnp.int32, (SEQ, SHARE), 0) * SLOTS + rank + 1
+    slot = jnp.where(from_block == s, slot, 0).astype(jnp.float32)
     token = listing - s * SPAN
-
-    def lanes(x, c):
-        return jnp.concatenate([x[j : j + 1] for j in range(c * step // SHARE, (c + 1) * step // SHARE)], axis=1)
-
+    token_iota = lax.broadcasted_iota(jnp.int32, (SPAN, SHARE), 0)
+    found = jnp.zeros((SPAN, SHARE), jnp.float32)
+    for j in range(SEQ):
+        found += jnp.where(token_iota == token[j : j + 1], slot[j : j + 1], 0.0)
+    found = jnp.sum(found, axis=1, keepdims=True) - 1.0
+    row = jnp.broadcast_to(found, (SPAN, 128)).T[0:1]
+    back_ref[...] = one_hot(lax.broadcasted_iota(jnp.int32, (SPAN, SPAN), 1).astype(jnp.float32) == found)
+    take = one_hot(lax.broadcasted_iota(jnp.int32, (SPAN, SPAN), 0).astype(jnp.float32) == row)
     step = 512
-    iota = lax.broadcasted_iota(jnp.int32, (SPAN, step), 0)
-    take = jnp.zeros((SPAN, SPAN), jnp.float32)
-    back = jnp.zeros((SPAN, SPAN), jnp.float32)
-    for c in range(KEPT // step):
-        a = one_hot(iota == lanes(slot, c))
-        b = one_hot(iota == lanes(token, c))
-        take += lax.dot_general(a, b, NT, preferred_element_type=jnp.float32)
-        back += lax.dot_general(b, a, NT, preferred_element_type=jnp.float32)
-    take = take.astype(jnp.bfloat16)
-    back_ref[...] = back.astype(jnp.bfloat16)
 
     def to_slots(i, ref):
         rows = jnp.dot(take, ref[...], preferred_element_type=jnp.float32).astype(jnp.bfloat16)
@@ -339,7 +334,7 @@
     def store_stat(i, t, value):
         wide = jnp.broadcast_to(value, (TILE, 128)).T
         for j in range(TILE // SHARE):
-            stats[me, i, pl.ds(2 * t + j, 1), :] = wide[0:1, j * SHARE : (j + 1) * SHARE]
+            stats[me, i, pl.ds(TILE // SHARE * t + j, 1), :] = wide[0:1, j * SHARE : (j + 1) * SHARE]
 
     def score_tile(t, _):
         query = tile_rows(1, t)
@@ -364,14 +359,17 @@
         return 0
 
     def spread_tile(t, rows):
-        tile_iota = lax.broadcasted_iota(jnp.int32, (2 * SLOTS * SEQ, TILE), 0)
+        tile_iota = lax.broadcasted_iota(jnp.int32, (SEQ * PART, TILE), 0)
         tile_codes = []
-        for j in range(2):
-            code = unit_codes(2 * t + j)
-            tile_codes.append((code >> 3) * (2 * SLOTS) + j * SLOTS + (code & 7))
+        for j in range(TILE // SHARE):
+            code = unit_codes(TILE // SHARE * t + j)
+            tile_codes.append((code >> 3) * PART + j * SLOTS + (code & 7))
         spread = one_hot(tile_iota == jnp.concatenate(tile_codes, axis=1))
         rows = jnp.dot(spread, rows.astype(jnp.bfloat16), preferred_element_type=jnp.float32)
-        return rows.astype(jnp.bfloat16).reshape(SEQ, 2 * SLOTS, HD)
+        return rows.astype(jnp.bfloat16).reshape(SEQ, PART, HD)
+
+    def part_of(t):
+        return pl.ds(pl.multiple_of(t * PART, PART), PART)
 
     def query_tile(t, _):
         grad = tile_rows(3, t)
@@ -391,12 +389,8 @@
         terms[0:8, :] += term
         store_stat(1, t, delta)
 
-        q_slots[:, pl.ds(pl.multiple_of(t * 2 * SLOTS, 16), 2 * SLOTS), :] = spread_tile(t, grads)
-
-        @pl.when((t & 1) == 1)
-        def _():
-            send_home(lambda i: q_home(t >> 1, i), 0)
-
+        q_slots[:, part_of(t), :] = spread_tile(t, grads)
+        send_home(lambda i: q_home(t, i), 0)
         return 0
 
 
@@ -413,19 +407,14 @@
             stat_copy(me, me ^ step).wait_send()
 
 
-    def q_home(half, i):
-        count = CHUNK // 2
-        return (
-            q_slots.at[i, pl.ds(pl.multiple_of(half * count, count), count), :],
-            home_ref.at[0, pl.ds(pl.multiple_of(seat * CHUNK + half * count, count), count), :],
-        )
-
-    def kv_home(half, i):
-        count = CHUNK // 2
-        return (
-            kv_slots.at[:, i, pl.ds(pl.multiple_of(half * count, count), count), :],
-            home_ref.at[1:3, pl.ds(pl.multiple_of(seat * CHUNK + half * count, count), count), :],
-        )
+    def home_rows(t):
+        return pl.ds(pl.multiple_of(seat * CHUNK + t * PART, PART), PART)
+
+    def q_home(t, i):
+        return q_slots.at[i, part_of(t), :], home_ref.at[0, home_rows(t), :]
+
+    def kv_home(t, i):
+        return kv_slots.at[:, i, part_of(t), :], home_ref.at[1:3, home_rows(t), :]
 
     def send_home(copies, sem):
         def start(n, _):
@@ -465,12 +454,8 @@
         grads, term = norm_grads(raw[0, local_rows(t), :], gain_k_ref[...], key_grad * SCALING)
         terms[8:16, :] += term
         for i, result in enumerate((grads, value_grad)):
-            kv_slots[i, :, pl.ds(pl.multiple_of(t * 2 * SLOTS, 16), 2 * SLOTS), :] = spread_tile(t, result)
-
-        @pl.when((t & 1) == 1)
-        def _():
-            send_home(lambda i: kv_home(t >> 1, i), 1)
-
+            kv_slots[i, :, part_of(t), :] = spread_tile(t, result)
+        send_home(lambda i: kv_home(t, i), 1)
         return 0
 
 

time: 120 us -> 122 us (1.017)
  Pallas kernels: 120 us -> 122 us
    pallas_call x1, Pallas kernels: 117 us -> 119 us  [core(): pl.pallas_call(core_kernel, name='core', in_specs=[in_vmem] * 7, out_spec...]
where the time goes in v6:
time: 122 us
  Pallas kernels  122 us (100%)
    pallas_call x1, Pallas kernels, core(): pl.pallas_call(core_kernel, name='core', in_specs=[in_vmem] * 7, out_spec...  119 us
    pallas_call x1, Pallas kernels, to_rows(): pl.pallas_call(rows_kernel, name='to_rows', grid=(parts,), in_specs=[pl.B...  2.8 us

profile of v6, /device:TPU:1, one launch (start us, length us, event | category | flops | bytes accessed | tf_op | source)
XLA Modules:
  0.0 122.2 jit_solution(3868493496048403591)
XLA Ops:
  0.6 118.7 %core.1 = (bf16[3,1536,128]{2,1,0:T(8,128)(2,1)}, bf16[256,256]{1,0:T(8,128)(2,1)}, f32[16,128]{1,0:T(8,128)}) custom-call(s32[32,128]{1,0:T(8,128)} %bitcast.13, bf16[256,768]{1,0:T(8,128)(2,1)} %bitcast.9, bf16[256,768]{1,0:T(8,128)(2,1)} %bitcast.10, bf16[256,768]{1,0:T(8,128)(2,1)} %bitcast.11, bf16[256,768]{1,0:T(8,128)(2,1)} %bitcast.12, ...), custom_call_target="tpu_custom_call" | custom-call | tf_op jit(solution)/shard_map/core/pallas_call | solution.py:574
  119.3 2.8 %to_rows.1 = (bf16[1,256,768]{2,1,0:T(8,128)(2,1)}, bf16[1,256,768]{2,1,0:T(8,128)(2,1)}, bf16[1,256,768]{2,1,0:T(8,128)(2,1)}, f32[1,128]{1,0:T(1,128)}, f32[1,128]{1,0:T(1,128)}) custom-call(bf16[256,256]{1,0:T(8,128)(2,1)} %get-tuple-element.13.back_ref, bf16[3,1536,128]{2,1,0:T(8,128)(2,1)} %get-tuple-element.14.slots_ref, ...), custom_call_target="tpu_custom_call" | custom-call | flops 300000000 | bytes 3000000 | tf_op jit(solution)/shard_map/to_rows/pallas_call | solution.py:638

commit v7 on v6

--- a/solution.py
+++ b/solution.py
@@ -216,7 +216,15 @@
     def chunk(ref, a, i):
         return ref.at[a, pl.ds(pl.multiple_of(i * CHUNK, 16), CHUNK), :]
 
-    turn = (3 * s) >> 2
+    def nth_target(n):
+        v = 3 * (s & 7) + 6 * (s >> 3) + 7 * n
+        return v - 24 * ((v * 171) >> 12)
+
+    def nth_source(n):
+        turn = n & 7
+        away = ((turn + 1) >> 1) * (2 * (turn & 1) - 1)
+        return (((s >> 3) + (n >> 3)) & 3) * 8 + (((s & 7) + away) & 7)
+
 
     def route(a, first, last, beside=None):
         def start(n, _):
@@ -228,8 +236,7 @@
                     def _():
                         piece(beside, n - first).start()
 
-            i = n + turn
-            i = jnp.where(i < TARGETS, i, i - TARGETS)
+            i = nth_target(n)
             there, own = target(i)
 
             @pl.when(jnp.logical_not(own))
@@ -418,7 +425,7 @@
 
     def send_home(copies, sem):
         def start(n, _):
-            i = (n + s) & (SEQ - 1)
+            i = nth_source(n)
             src, dst = copies(i)
 
             @pl.when(jnp.logical_not(to_self(i)))

time: 122 us -> 121 us (level)
  Pallas kernels: 122 us -> 120 us
where the time goes in v7:
time: 121 us
  Pallas kernels  120 us (99%)
    pallas_call x1, Pallas kernels, core(): pl.pallas_call(core_kernel, name='core', in_specs=[in_vmem] * 7, out_spec...  118 us
    pallas_call x1, Pallas kernels, to_rows(): pl.pallas_call(rows_kernel, name='to_rows', grid=(parts,), in_specs=[pl.B...  2.8 us

profile of v7, /device:TPU:1, one launch (start us, length us, event | category | flops | bytes accessed | tf_op | source)
XLA Modules:
  0.0 121.1 jit_solution(9235916823652926461)
XLA Ops:
  0.6 117.6 %core.1 = (bf16[3,1536,128]{2,1,0:T(8,128)(2,1)}, bf16[256,256]{1,0:T(8,128)(2,1)}, f32[16,128]{1,0:T(8,128)}) custom-call(s32[32,128]{1,0:T(8,128)} %bitcast.13, bf16[256,768]{1,0:T(8,128)(2,1)} %bitcast.9, bf16[256,768]{1,0:T(8,128)(2,1)} %bitcast.10, bf16[256,768]{1,0:T(8,128)(2,1)} %bitcast.11, bf16[256,768]{1,0:T(8,128)(2,1)} %bitcast.12, ...), custom_call_target="tpu_custom_call" | custom-call | tf_op jit(solution)/shard_map/core/pallas_call | solution.py:581
  118.2 2.8 %to_rows.1 = (bf16[1,256,768]{2,1,0:T(8,128)(2,1)}, bf16[1,256,768]{2,1,0:T(8,128)(2,1)}, bf16[1,256,768]{2,1,0:T(8,128)(2,1)}, f32[1,128]{1,0:T(1,128)}, f32[1,128]{1,0:T(1,128)}) custom-call(bf16[256,256]{1,0:T(8,128)(2,1)} %get-tuple-element.13.back_ref, bf16[3,1536,128]{2,1,0:T(8,128)(2,1)} %get-tuple-element.14.slots_ref, ...), custom_call_target="tpu_custom_call" | custom-call | flops 300000000 | bytes 3000000 | tf_op jit(solution)/shard_map/to_rows/pallas_call | solution.py:645

commit v8 on v6

--- a/solution.py
+++ b/solution.py
@@ -26,7 +26,6 @@
 TILE = 512
 PART = TILE // SHARE * SLOTS
 TILES = ROWS // TILE
-PIECE = 128
 SCALING = 1.0 / math.sqrt(HD)
 LOG2E = 1.4426950408889634
 VMEM_LIMIT = 56 * 1024 * 1024
@@ -126,17 +125,37 @@
     sibling = (1 - dp, s, x)
     corner = dp * 4 + x
     same = active & (clip == dp)
-    own_source = jnp.where(same, s, -1)
-    own_target = jnp.where(same, seat, -1)
-
-    def to_self(i):
-        return i == own_source
+
+    first_target = jnp.where(same, seat, 3 * (s & 7) + 6 * (s >> 3))
+
+    def nth_target(n):
+        v = first_target + 7 * n
+        return v - TARGETS * ((v * 171) >> 12)
+
+    def nth_source(n):
+        turn = n & 7
+        away = ((turn + 1) >> 1) * (2 * (turn & 1) - 1)
+        return (((s >> 3) + (n >> 3)) & 3) * 8 + (((s & 7) + away) & 7)
 
     def target(i):
-        return place(dp, i) + (x,), i == own_target
+        return place(dp, i) + (x,)
 
     def source(i):
         return (clip, i, x)
+
+    def each(count, act, act_self=None):
+        @pl.when(jnp.logical_not(same))
+        def _():
+            act(0)
+
+        if act_self is not None:
+            pl.when(same)(act_self)
+
+        def step(n, _):
+            act(n)
+            return 0
+
+        lax.fori_loop(1, count, step, 0, unroll=count - 1)
 
     def member(i):
         return (i & 1, (s & 23) + 8 * (i >> 1), x)
@@ -152,37 +171,19 @@
     def greet_device(there):
         pl.semaphore_signal(barrier, inc=1, device_id=there, device_id_type=MESH)
 
-    def greet_target(i, _):
-        there, own = target(i)
-
-        @pl.when(jnp.logical_not(own))
-        def _():
-            greet_device(there)
-
-        return 0
-
-    def greet_source(i, _):
-        @pl.when(jnp.logical_not(to_self(i)))
-        def _():
-            greet_device(source(i))
-
-        return 0
-
-    def greet_corner(i, _):
-        @pl.when(i != corner)
-        def _():
-            greet_device((i >> 2, s, i & 3))
-
-        return 0
-
     @pl.when(active)
     def _():
-        lax.fori_loop(0, SEQ, greet_source, 0)
+        each(SEQ, lambda n: greet_device(source(nth_source(n))))
         for step in (1, 2, 3):
             greet_device(member(me ^ step))
 
-    lax.fori_loop(0, TARGETS, greet_target, 0)
-    lax.fori_loop(0, 8, greet_corner, 0)
+    each(TARGETS, lambda n: greet_device(target(nth_target(n))))
+
+    def at_corner(i):
+        return (i >> 2, s, i & 3)
+
+    for step in range(1, 8):
+        greet_device(at_corner(corner ^ step))
 
 
     listing = list_ref[...]
@@ -216,42 +217,19 @@
     def chunk(ref, a, i):
         return ref.at[a, pl.ds(pl.multiple_of(i * CHUNK, 16), CHUNK), :]
 
-    turn = (3 * s) >> 2
-
-    def route(a, first, last, beside=None):
-        def start(n, _):
-            if beside is not None:
-
-                @pl.when(n < first + ROWS // PIECE)
-                def _():
-                    @pl.when(active)
-                    def _():
-                        piece(beside, n - first).start()
-
-            i = n + turn
-            i = jnp.where(i < TARGETS, i, i - TARGETS)
-            there, own = target(i)
-
-            @pl.when(jnp.logical_not(own))
-            def _():
-                remote(chunk(slots, a, i), chunk(arrived, a, s), route_send.at[a], route_recv.at[a], there).start()
-
-            return 0
-
-        lax.fori_loop(first, last, start, 0)
-
-        if last == TARGETS:
-
-            @pl.when(same)
-            def _():
-                pltpu.make_async_copy(chunk(slots, a, seat), chunk(arrived, a, s), route_recv.at[a]).start()
+    def route(a):
+        def start(n):
+            i = nth_target(n)
+            there = target(i)
+            remote(chunk(slots, a, i), chunk(arrived, a, s), route_send.at[a], route_recv.at[a], there).start()
+
+        def start_self():
+            pltpu.make_async_copy(chunk(slots, a, seat), chunk(arrived, a, s), route_recv.at[a]).start()
+
+        each(TARGETS, start, start_self)
 
     def rows_of(a, i):
         return full.at[a, pl.ds(pl.multiple_of(i * ROWS, ROWS), ROWS), :]
-
-    def piece(a, n):
-        rows = full.at[a, pl.ds(pl.multiple_of(me * ROWS + n * PIECE, PIECE), PIECE), :]
-        return remote(rows, rows, near_send.at[a, 0], near_recv.at[a, 0], member(me ^ 2))
 
     to_slots(0, k_ref)
     arrivals = jnp.where(active, SEQ + 3, 0) - jnp.where(same, 2, 0)
@@ -262,9 +240,9 @@
     def _():
         exchange.start()
 
-    route(0, 0, TARGETS)
+    route(0)
     to_slots(1, q_ref)
-    route(1, 0, TARGETS)
+    route(1)
     to_slots(2, v_ref)
     to_slots(3, g_ref)
 
@@ -287,13 +265,6 @@
     def near(a, way, rows, there):
         return remote(rows_of(a, rows), rows_of(a, rows), near_send.at[a, way], near_recv.at[a, way], member(there))
 
-    def gather_rest():
-        def start(n, _):
-            piece(3, n).start()
-            return 0
-
-        lax.fori_loop(0, ROWS // PIECE, start, 0)
-
     def gather_pass(a):
         near(a, 0, me ^ 2, me).wait_recv()
         near(a, 2, me ^ 2, me ^ 1).start()
@@ -317,6 +288,7 @@
             gain = (gain_k_ref, gain_q_ref)[a][...]
             rows = rows * inverse_norm(rows) * gain
         full[a, own_rows, :] = rows.astype(jnp.bfloat16)
+        near(a, 0, me, me ^ 2).start()
         near(a, 1, me, me ^ 1).start()
 
 
@@ -390,7 +362,6 @@
         store_stat(1, t, delta)
 
         q_slots[:, part_of(t), :] = spread_tile(t, grads)
-        send_home(lambda i: q_home(t, i), 0)
         return 0
 
 
@@ -410,29 +381,23 @@
     def home_rows(t):
         return pl.ds(pl.multiple_of(seat * CHUNK + t * PART, PART), PART)
 
-    def q_home(t, i):
-        return q_slots.at[i, part_of(t), :], home_ref.at[0, home_rows(t), :]
+    def q_home(i):
+        return q_slots.at[i], home_ref.at[0, pl.ds(pl.multiple_of(seat * CHUNK, CHUNK), CHUNK), :]
 
     def kv_home(t, i):
         return kv_slots.at[:, i, part_of(t), :], home_ref.at[1:3, home_rows(t), :]
 
     def send_home(copies, sem):
-        def start(n, _):
-            i = (n + s) & (SEQ - 1)
+        def start(n):
+            i = nth_source(n)
             src, dst = copies(i)
-
-            @pl.when(jnp.logical_not(to_self(i)))
-            def _():
-                remote(src, dst, home_send.at[sem], home_recv.at[sem], source(i)).start()
-
-            return 0
-
-        lax.fori_loop(0, SEQ, start, 0)
-
-        @pl.when(same)
-        def _():
+            remote(src, dst, home_send.at[sem], home_recv.at[sem], source(i)).start()
+
+        def start_self():
             src, dst = copies(s)
             pltpu.make_async_copy(src, dst, home_recv.at[sem]).start()
+
+        each(SEQ, start, start_self)
 
 
     def stat_row(i, cols):
@@ -459,25 +424,24 @@
         return 0
 
 
-    def part_start(i, _):
-        @pl.when(jnp.logical_not(to_self(i)))
-        def _():
-            remote(terms, parts.at[seat], part_sem.at[0], part_sem.at[1], source(i)).start()
-
-        return 0
+    def part_start(n):
+        remote(terms, parts.at[seat], part_sem.at[0], part_sem.at[1], source(nth_source(n))).start()
+
+    def part_self():
+        pltpu.make_async_copy(terms, parts.at[seat], part_sem.at[1]).start()
 
     @pl.when(active)
     def _():
         build_pick()
         to_dense(0)
 
-    route(2, 0, TARGETS, beside=0)
+    route(2)
 
     @pl.when(active)
     def _():
         to_dense(1)
 
-    route(3, 0, TARGETS // 2, beside=1)
+    route(3)
 
     @pl.when(active)
     def _():
@@ -486,54 +450,33 @@
         gather_finish(0)
         lax.fori_loop(0, TILES // 2, score_tile, 0)
         to_dense(2)
-
-    route(3, TARGETS // 2, TARGETS, beside=2)
-
-    @pl.when(active)
-    def _():
         gather_pass(1)
         lax.fori_loop(TILES // 2, TILES, score_tile, 0)
         gather_pass(2)
         to_dense(3)
-        gather_rest()
         gather_finish(2)
         lax.fori_loop(0, TILES, query_tile, 0)
         stat_start()
         gather_pass(3)
+        send_home(q_home, 0)
         gather_finish(1)
         gather_finish(3)
         stat_finish()
         lax.fori_loop(0, TILES, key_tile, 0)
-        lax.fori_loop(0, SEQ, part_start, 0)
-
-        @pl.when(same)
-        def _():
-            pltpu.make_async_copy(terms, parts.at[seat], part_sem.at[1]).start()
+        each(SEQ, part_start, part_self)
 
     remote(parts, parts, part_sem.at[0], part_sem.at[1], sibling).wait_recv()
     partial[...] = jnp.sum(parts[...], axis=0)
 
     def cross_copy(i, dst):
-        return remote(partial, cross.at[dst], cross_send.at[i], cross_recv.at[dst], (i >> 2, s, i & 3))
-
-    def cross_start(i, _):
-        @pl.when(i != corner)
-        def _():
-            cross_copy(i, corner).start()
-
-        return 0
-
-    def cross_finish(i, _):
-        @pl.when(i != corner)
-        def _():
-            cross_copy(i, i).wait_recv()
-            cross_copy(i, corner).wait_send()
-
-        return 0
+        return remote(partial, cross.at[dst], cross_send.at[i], cross_recv.at[dst], at_corner(i))
 
     cross[pl.ds(corner, 1)] = partial[...][None]
-    lax.fori_loop(0, 8, cross_start, 0)
-    lax.fori_loop(0, 8, cross_finish, 0)
+    for step in range(1, 8):
+        cross_copy(corner ^ step, corner).start()
+    for step in range(1, 8):
+        cross_copy(corner ^ step, corner ^ step).wait_recv()
+        cross_copy(corner ^ step, corner).wait_send()
     total_ref[...] = jnp.sum(cross[...], axis=0)
 
 

time: 122 us -> 125 us (1.025)
  Pallas kernels: 122 us -> 124 us
    pallas_call x1, Pallas kernels: 119 us -> 121 us  [core(): pl.pallas_call(core_kernel, name='core', in_specs=[in_vmem] * 7, out_spec...]
where the time goes in v8:
time: 125 us
  Pallas kernels  124 us (99%)
    pallas_call x1, Pallas kernels, core(): pl.pallas_call(core_kernel, name='core', in_specs=[in_vmem] * 7, out_spec...  121 us
    pallas_call x1, Pallas kernels, to_rows(): pl.pallas_call(rows_kernel, name='to_rows', grid=(parts,), in_specs=[pl.B...  2.8 us

profile of v8, /device:TPU:1, one launch (start us, length us, event | category | flops | bytes accessed | tf_op | source)
XLA Modules:
  0.0 124.9 jit_solution(10917823751416482501)
XLA Ops:
  0.6 121.5 %core.1 = (bf16[3,1536,128]{2,1,0:T(8,128)(2,1)}, bf16[256,256]{1,0:T(8,128)(2,1)}, f32[16,128]{1,0:T(8,128)}) custom-call(s32[32,128]{1,0:T(8,128)} %bitcast.13, bf16[256,768]{1,0:T(8,128)(2,1)} %bitcast.9, bf16[256,768]{1,0:T(8,128)(2,1)} %bitcast.10, bf16[256,768]{1,0:T(8,128)(2,1)} %bitcast.11, bf16[256,768]{1,0:T(8,128)(2,1)} %bitcast.12, ...), custom_call_target="tpu_custom_call" | custom-call | tf_op jit(solution)/shard_map/core/pallas_call | solution.py:517
  122.1 2.8 %to_rows.1 = (bf16[1,256,768]{2,1,0:T(8,128)(2,1)}, bf16[1,256,768]{2,1,0:T(8,128)(2,1)}, bf16[1,256,768]{2,1,0:T(8,128)(2,1)}, f32[1,128]{1,0:T(1,128)}, f32[1,128]{1,0:T(1,128)}) custom-call(bf16[256,256]{1,0:T(8,128)(2,1)} %get-tuple-element.13.back_ref, bf16[3,1536,128]{2,1,0:T(8,128)(2,1)} %get-tuple-element.14.slots_ref, ...), custom_call_target="tpu_custom_call" | custom-call | flops 300000000 | bytes 3000000 | tf_op jit(solution)/shard_map/to_rows/pallas_call | solution.py:581

commit v9 on v8

--- a/solution.py
+++ b/solution.py
@@ -20,7 +20,6 @@
 CHUNK = UNITS * SLOTS
 MEMBERS = 4
 TARGETS = HEAD_PART * MEMBERS
-OUT = TARGETS * CHUNK
 FLAT = SEQ * CHUNK
 KEPT = SEQ * SHARE
 TILE = 512
@@ -84,11 +83,16 @@
     g_ref,
     gain_q_ref,
     gain_k_ref,
-    home_ref,
+    home_q_ref,
+    home_kv_ref,
     back_ref,
     total_ref,
-    slots,
-    arrived,
+    slots_kq,
+    slots_v,
+    slots_g,
+    arrived_kq,
+    arrived_v,
+    arrived_g,
     enc_ref,
     other,
     codes,
@@ -155,7 +159,7 @@
             act(n)
             return 0
 
-        lax.fori_loop(1, count, step, 0, unroll=count - 1)
+        lax.fori_loop(1, count, step, 0)
 
     def member(i):
         return (i & 1, (s & 23) + 8 * (i >> 1), x)
@@ -209,29 +213,34 @@
     take = one_hot(lax.broadcasted_iota(jnp.int32, (SPAN, SPAN), 0).astype(jnp.float32) == row)
     step = 512
 
-    def to_slots(i, ref):
+    slots = (slots_kq, slots_v, slots_g)
+    arrived = (arrived_kq, arrived_v, arrived_g)
+
+    def to_slots(part, i, ref):
         rows = jnp.dot(take, ref[...], preferred_element_type=jnp.float32).astype(jnp.bfloat16)
         for h in range(HEAD_PART):
-            slots[i, h * SPAN : (h + 1) * SPAN, :] = rows[:, h * HD : (h + 1) * HD]
-
-    def chunk(ref, a, i):
-        return ref.at[a, pl.ds(pl.multiple_of(i * CHUNK, 16), CHUNK), :]
-
-    def route(a):
+            quarters = rows[:, h * HD : (h + 1) * HD].reshape(MEMBERS, CHUNK, HD)
+            slots[part][h * MEMBERS : (h + 1) * MEMBERS, i] = quarters
+
+    def route(part):
         def start(n):
             i = nth_target(n)
-            there = target(i)
-            remote(chunk(slots, a, i), chunk(arrived, a, s), route_send.at[a], route_recv.at[a], there).start()
+            src, dst = slots[part].at[i], arrived[part].at[s]
+            remote(src, dst, route_send.at[part], route_recv.at[part], target(i)).start()
 
         def start_self():
-            pltpu.make_async_copy(chunk(slots, a, seat), chunk(arrived, a, s), route_recv.at[a]).start()
+            pltpu.make_async_copy(slots[part].at[seat], arrived[part].at[s], route_recv.at[part]).start()
 
         each(TARGETS, start, start_self)
+
+    def arrive(part):
+        remote(arrived[part], arrived[part], route_send.at[part], route_recv.at[part], sibling).wait_recv()
 
     def rows_of(a, i):
         return full.at[a, pl.ds(pl.multiple_of(i * ROWS, ROWS), ROWS), :]
 
-    to_slots(0, k_ref)
+    to_slots(0, 0, k_ref)
+    to_slots(0, 1, q_ref)
     arrivals = jnp.where(active, SEQ + 3, 0) - jnp.where(same, 2, 0)
     pl.semaphore_wait(barrier, TARGETS + 7 + arrivals)
     exchange = remote(enc_ref, other, enc_sem.at[0], enc_sem.at[1], sibling)
@@ -241,10 +250,9 @@
         exchange.start()
 
     route(0)
-    to_slots(1, q_ref)
+    to_slots(1, 0, v_ref)
     route(1)
-    to_slots(2, v_ref)
-    to_slots(3, g_ref)
+    to_slots(2, 0, g_ref)
 
 
     def unit_codes(u):
@@ -281,8 +289,9 @@
     own_rows = pl.ds(pl.multiple_of(me * ROWS, 256), ROWS)
 
     def to_dense(a):
-        remote(arrived.at[a], arrived.at[a], route_send.at[a], route_recv.at[a], sibling).wait_recv()
-        rows = jnp.dot(pick[...], arrived[a], preferred_element_type=jnp.float32)
+        part, i = ((0, 0), (0, 1), (1, 0), (2, 0))[a]
+        rows = arrived[part][:, i].reshape(FLAT, HD)
+        rows = jnp.dot(pick[...], rows, preferred_element_type=jnp.float32)
         if a < 2:
             raw[a] = rows.astype(jnp.bfloat16)
             gain = (gain_k_ref, gain_q_ref)[a][...]
@@ -378,14 +387,11 @@
             stat_copy(me, me ^ step).wait_send()
 
 
-    def home_rows(t):
-        return pl.ds(pl.multiple_of(seat * CHUNK + t * PART, PART), PART)
-
     def q_home(i):
-        return q_slots.at[i], home_ref.at[0, pl.ds(pl.multiple_of(seat * CHUNK, CHUNK), CHUNK), :]
+        return q_slots.at[i], home_q_ref.at[seat]
 
     def kv_home(t, i):
-        return kv_slots.at[:, i, part_of(t), :], home_ref.at[1:3, home_rows(t), :]
+        return kv_slots.at[t, i], home_kv_ref.at[seat, t]
 
     def send_home(copies, sem):
         def start(n):
@@ -419,7 +425,7 @@
         grads, term = norm_grads(raw[0, local_rows(t), :], gain_k_ref[...], key_grad * SCALING)
         terms[8:16, :] += term
         for i, result in enumerate((grads, value_grad)):
-            kv_slots[i, :, part_of(t), :] = spread_tile(t, result)
+            kv_slots[t, :, i] = spread_tile(t, result)
         send_home(lambda i: kv_home(t, i), 1)
         return 0
 
@@ -433,26 +439,24 @@
     @pl.when(active)
     def _():
         build_pick()
+        arrive(0)
         to_dense(0)
 
     route(2)
-
-    @pl.when(active)
-    def _():
-        to_dense(1)
-
-    route(3)
 
     @pl.when(active)
     def _():
         terms[...] = jnp.zeros_like(terms)
+        to_dense(1)
         gather_pass(0)
         gather_finish(0)
         lax.fori_loop(0, TILES // 2, score_tile, 0)
+        arrive(1)
         to_dense(2)
         gather_pass(1)
         lax.fori_loop(TILES // 2, TILES, score_tile, 0)
         gather_pass(2)
+        arrive(2)
         to_dense(3)
         gather_finish(2)
         lax.fori_loop(0, TILES, query_tile, 0)
@@ -481,9 +485,9 @@
 
 
     def sent(targets, sources):
-        for a in range(4):
-            rows = slots.at[a, 0 : targets * CHUNK, :]
-            remote(rows, rows, route_send.at[a], route_recv.at[a], sibling).wait_send()
+        for part in range(3):
+            rows = slots[part].at[0:targets]
+            remote(rows, rows, route_send.at[part], route_recv.at[part], sibling).wait_send()
         if sources:
             for a in range(4):
                 gather_sent(a)
@@ -506,8 +510,8 @@
     def _():
         sent(TARGETS, 0)
 
-    remote(home_ref.at[0], home_ref.at[0], home_send.at[0], home_recv.at[0], sibling).wait_recv()
-    remote(home_ref.at[1:3], home_ref.at[1:3], home_send.at[1], home_recv.at[1], sibling).wait_recv()
+    remote(home_q_ref, home_q_ref, home_send.at[0], home_recv.at[0], sibling).wait_recv()
+    remote(home_kv_ref, home_kv_ref, home_send.at[1], home_recv.at[1], sibling).wait_recv()
 
 
 def core(listing, k, q, v, g, gain_q, gain_k):
@@ -518,15 +522,20 @@
         core_kernel,
         name="core",
         in_specs=[in_vmem] * 7,
-        out_specs=[pl.BlockSpec(memory_space=pl.ANY), in_vmem, in_vmem],
+        out_specs=[pl.BlockSpec(memory_space=pl.ANY)] * 2 + [in_vmem] * 2,
         out_shape=(
-            jax.ShapeDtypeStruct((3, OUT, HD), bf16),
+            jax.ShapeDtypeStruct((TARGETS, CHUNK, HD), bf16),
+            jax.ShapeDtypeStruct((TARGETS, TILES, 2, PART, HD), bf16),
             jax.ShapeDtypeStruct((SPAN, SPAN), bf16),
             jax.ShapeDtypeStruct((16, HD), f32),
         ),
         scratch_shapes=[
-            pltpu.VMEM((4, OUT, HD), bf16),
-            pltpu.VMEM((4, FLAT, HD), bf16),
+            pltpu.VMEM((TARGETS, 2, CHUNK, HD), bf16),
+            pltpu.VMEM((TARGETS, 1, CHUNK, HD), bf16),
+            pltpu.VMEM((TARGETS, 1, CHUNK, HD), bf16),
+            pltpu.VMEM((SEQ, 2, CHUNK, HD), bf16),
+            pltpu.VMEM((SEQ, 1, CHUNK, HD), bf16),
+            pltpu.VMEM((SEQ, 1, CHUNK, HD), bf16),
             pltpu.VMEM((SEQ, SHARE), jnp.int32),
             pltpu.VMEM((SEQ, SHARE), jnp.int32),
             pltpu.VMEM((SEQ, SHARE), jnp.int32),
@@ -537,7 +546,7 @@
             pltpu.VMEM((TILE, KEPT), f32),
             pltpu.VMEM((ROWS, 128), f32),
             pltpu.VMEM((SEQ, CHUNK, HD), bf16),
-            pltpu.VMEM((2, SEQ, CHUNK, HD), bf16),
+            pltpu.VMEM((TILES, SEQ, 2, PART, HD), bf16),
             pltpu.VMEM((MEMBERS, 2, 8, SHARE), f32),
             pltpu.VMEM((16, HD), f32),
             pltpu.VMEM((SEQ, 16, HD), f32),
@@ -545,8 +554,8 @@
             pltpu.VMEM((16, HD), f32),
             pltpu.VMEM((8, 16, HD), f32),
             dma((2,)),
-            dma((4,)),
-            dma((4,)),
+            dma((3,)),
+            dma((3,)),
             dma((4, 3)),
             dma((4, 3)),
             dma((MEMBERS,)),
@@ -563,17 +572,21 @@
     )(listing, k, q, v, g, gain_q, gain_k)
 
 
-def rows_kernel(back_ref, slots_ref, total_ref, q_ref, k_ref, v_ref, gain_q_ref, gain_k_ref):
-    for i, ref in enumerate((q_ref, k_ref, v_ref)):
-        for h in range(slots_ref.shape[1] // SPAN):
-            rows = slots_ref[i, h * SPAN : (h + 1) * SPAN, :]
-            rows = jnp.dot(back_ref[...], rows, preferred_element_type=jnp.float32)
+def rows_kernel(back_ref, home_q_ref, home_kv_ref, total_ref, q_ref, k_ref, v_ref, gain_q_ref, gain_k_ref):
+    for h in range(home_q_ref.shape[0] // MEMBERS):
+        seats = slice(h * MEMBERS, (h + 1) * MEMBERS)
+        for ref, rows in (
+            (q_ref, home_q_ref[seats]),
+            (k_ref, home_kv_ref[seats, :, 0]),
+            (v_ref, home_kv_ref[seats, :, 1]),
+        ):
+            rows = jnp.dot(back_ref[...], rows.reshape(SPAN, HD), preferred_element_type=jnp.float32)
             ref[0, :, h * HD : (h + 1) * HD] = rows.astype(jnp.bfloat16)
     gain_q_ref[...] = jnp.sum(total_ref[0:8, :], axis=0, keepdims=True)
     gain_k_ref[...] = jnp.sum(total_ref[8:16, :], axis=0, keepdims=True)
 
 
-def to_rows(back, slots, total):
+def to_rows(back, home_q, home_kv, total):
     width = HEAD_PART * HD
     parts = 2
     big = jax.ShapeDtypeStruct((1, SPAN, width), jnp.bfloat16)
@@ -584,7 +597,8 @@
         grid=(parts,),
         in_specs=[
             pl.BlockSpec((SPAN, SPAN), lambda h: (0, 0)),
-            pl.BlockSpec((3, OUT // parts, HD), lambda h: (0, h, 0)),
+            pl.BlockSpec((TARGETS // parts, CHUNK, HD), lambda h: (h, 0, 0)),
+            pl.BlockSpec((TARGETS // parts, TILES, 2, PART, HD), lambda h: (h, 0, 0, 0, 0)),
             pl.BlockSpec((16, HD), lambda h: (0, 0)),
         ],
         out_specs=[pl.BlockSpec((1, SPAN, width // parts), lambda h: (0, 0, h))] * 3
@@ -592,11 +606,11 @@
         out_shape=(big, big, big, small, small),
         compiler_params=pltpu.CompilerParams(vmem_limit_bytes=VMEM_LIMIT),
         cost_estimate=pl.CostEstimate(flops=3 * 10**8, bytes_accessed=3 * 10**6, transcendentals=0),
-    )(back, slots, total)
+    )(back, home_q, home_kv, total)
 
 
 def on_device(q_raw, k_raw, v_raw, out_grad, gain_q, gain_k, keep_list):
-    home, back, total = core(
+    home_q, home_kv, back, total = core(
         keep_list.reshape(SEQ, SHARE),
         k_raw[0],
         q_raw[0],
@@ -605,7 +619,7 @@
         gain_q.reshape(1, HD),
         gain_k.reshape(1, HD),
     )
-    q_out, k_out, v_out, gain_q_grad, gain_k_grad = to_rows(back, home, total)
+    q_out, k_out, v_out, gain_q_grad, gain_k_grad = to_rows(back, home_q, home_kv, total)
     return q_out, k_out, v_out, gain_q_grad.reshape(HD), gain_k_grad.reshape(HD)
 
 

time: 125 us -> 132 us (1.056)
  Pallas kernels: 124 us -> 131 us
    pallas_call x1, Pallas kernels: 121 us -> 128 us  [core(): pl.pallas_call(core_kernel, name='core', in_specs=[in_vmem] * 7, out_spec...]
where the time goes in v9:
time: 132 us
  Pallas kernels  131 us (99%)
    pallas_call x1, Pallas kernels, core(): pl.pallas_call(core_kernel, name='core', in_specs=[in_vmem] * 7, out_spec...  128 us
    pallas_call x1, Pallas kernels, to_rows(): pl.pallas_call(rows_kernel, name='to_rows', grid=(parts,), in_specs=[pl.B...  2.85 us

profile of v9, /device:TPU:1, one launch (start us, length us, event | category | flops | bytes accessed | tf_op | source)
XLA Modules:
  0.0 131.6 jit_solution(9579216602535599823)
XLA Ops:
  0.6 128.1 %core.1 = (bf16[24,64,128]{2,1,0:T(8,128)(2,1)}, bf16[24,2,2,32,128]{4,3,2,1,0:T(8,128)(2,1)}, bf16[256,256]{1,0:T(8,128)(2,1)}, f32[16,128]{1,0:T(8,128)}) custom-call(s32[32,128]{1,0:T(8,128)} %bitcast.13, bf16[256,768]{1,0:T(8,128)(2,1)} %bitcast.9, bf16[256,768]{1,0:T(8,128)(2,1)} %bitcast.10, bf16[256,768]{1,0:T(8,128)(2,1)} %bitcast.11, ...), custom_call_target="tpu_custom_call" | custom-call | tf_op jit(solution)/shard_map/core/pallas_call | solution.py:521
  128.7 2.9 %to_rows.1 = (bf16[1,256,768]{2,1,0:T(8,128)(2,1)}, bf16[1,256,768]{2,1,0:T(8,128)(2,1)}, bf16[1,256,768]{2,1,0:T(8,128)(2,1)}, f32[1,128]{1,0:T(1,128)}, f32[1,128]{1,0:T(1,128)}) custom-call(bf16[256,256]{1,0:T(8,128)(2,1)} %get-tuple-element.14.back_ref, bf16[24,64,128]{2,1,0:T(8,128)(2,1)} %get-tuple-element.15.home_q_ref, ...), custom_call_target="tpu_custom_call" | custom-call | flops 300000000 | bytes 3000000 | tf_op jit(solution)/shard_map/to_rows/pallas_call | solution.py:594

commit v10 on v7

--- a/solution.py
+++ b/solution.py
@@ -23,7 +23,7 @@
 OUT = TARGETS * CHUNK
 FLAT = SEQ * CHUNK
 KEPT = SEQ * SHARE
-TILE = 512
+TILE = 256
 PART = TILE // SHARE * SLOTS
 TILES = ROWS // TILE
 PIECE = 128
@@ -271,7 +271,7 @@
 
     route(0, 0, TARGETS)
     to_slots(1, q_ref)
-    route(1, 0, TARGETS)
+    route(1, 0, TARGETS // 2)
     to_slots(2, v_ref)
     to_slots(3, g_ref)
 
@@ -397,7 +397,11 @@
         store_stat(1, t, delta)
 
         q_slots[:, part_of(t), :] = spread_tile(t, grads)
-        send_home(lambda i: q_home(t, i), 0)
+
+        @pl.when((t & 1) == 1)
+        def _():
+            send_home(lambda i: q_home(t >> 1, i), 0)
+
         return 0
 
 
@@ -414,14 +418,19 @@
             stat_copy(me, me ^ step).wait_send()
 
 
-    def home_rows(t):
-        return pl.ds(pl.multiple_of(seat * CHUNK + t * PART, PART), PART)
-
-    def q_home(t, i):
-        return q_slots.at[i, part_of(t), :], home_ref.at[0, home_rows(t), :]
-
-    def kv_home(t, i):
-        return kv_slots.at[:, i, part_of(t), :], home_ref.at[1:3, home_rows(t), :]
+    half = CHUNK // 2
+
+    def half_of(h):
+        return pl.ds(pl.multiple_of(h * half, half), half)
+
+    def home_half(h):
+        return pl.ds(pl.multiple_of(seat * CHUNK + h * half, half), half)
+
+    def q_home(h, i):
+        return q_slots.at[i, half_of(h), :], home_ref.at[0, home_half(h), :]
+
+    def kv_home(h, i):
+        return kv_slots.at[:, i, half_of(h), :], home_ref.at[1:3, home_half(h), :]
 
     def send_home(copies, sem):
         def start(n, _):
@@ -462,7 +471,11 @@
         terms[8:16, :] += term
         for i, result in enumerate((grads, value_grad)):
             kv_slots[i, :, part_of(t), :] = spread_tile(t, result)
-        send_home(lambda i: kv_home(t, i), 1)
+
+        @pl.when((t & 1) == 1)
+        def _():
+            send_home(lambda i: kv_home(t >> 1, i), 1)
+
         return 0
 
 
@@ -478,28 +491,30 @@
         build_pick()
         to_dense(0)
 
-    route(2, 0, TARGETS, beside=0)
+    route(1, TARGETS // 2, TARGETS, beside=0)
+    route(2, 0, TARGETS)
 
     @pl.when(active)
     def _():
+        terms[...] = jnp.zeros_like(terms)
         to_dense(1)
-
-    route(3, 0, TARGETS // 2, beside=1)
-
-    @pl.when(active)
-    def _():
-        terms[...] = jnp.zeros_like(terms)
         gather_pass(0)
         gather_finish(0)
-        lax.fori_loop(0, TILES // 2, score_tile, 0)
+        lax.fori_loop(0, 1, score_tile, 0)
+
+    route(3, 0, TARGETS // 2, beside=1)
+
+    @pl.when(active)
+    def _():
+        lax.fori_loop(1, TILES // 2, score_tile, 0)
         to_dense(2)
 
     route(3, TARGETS // 2, TARGETS, beside=2)
 
     @pl.when(active)
     def _():
+        lax.fori_loop(TILES // 2, TILES, score_tile, 0)
         gather_pass(1)
-        lax.fori_loop(TILES // 2, TILES, score_tile, 0)
         gather_pass(2)
         to_dense(3)
         gather_rest()

time: 121 us -> 124 us (1.025)
  Pallas kernels: 120 us -> 123 us
    pallas_call x1, Pallas kernels: 118 us -> 121 us  [core(): pl.pallas_call(core_kernel, name='core', in_specs=[in_vmem] * 7, out_spec...]
where the time goes in v10:
time: 124 us
  Pallas kernels  123 us (99%)
    pallas_call x1, Pallas kernels, core(): pl.pallas_call(core_kernel, name='core', in_specs=[in_vmem] * 7, out_spec...  121 us
    pallas_call x1, Pallas kernels, to_rows(): pl.pallas_call(rows_kernel, name='to_rows', grid=(parts,), in_specs=[pl.B...  2.8 us

profile of v10, /device:TPU:1, one launch (start us, length us, event | category | flops | bytes accessed | tf_op | source)
XLA Modules:
  0.0 124.0 jit_solution(16290724662037316190)
XLA Ops:
  0.6 120.5 %core.1 = (bf16[3,1536,128]{2,1,0:T(8,128)(2,1)}, bf16[256,256]{1,0:T(8,128)(2,1)}, f32[16,128]{1,0:T(8,128)}) custom-call(s32[32,128]{1,0:T(8,128)} %bitcast.13, bf16[256,768]{1,0:T(8,128)(2,1)} %bitcast.9, bf16[256,768]{1,0:T(8,128)(2,1)} %bitcast.10, bf16[256,768]{1,0:T(8,128)(2,1)} %bitcast.11, bf16[256,768]{1,0:T(8,128)(2,1)} %bitcast.12, ...), custom_call_target="tpu_custom_call" | custom-call | tf_op jit(solution)/shard_map/core/pallas_call | solution.py:596
  121.2 2.8 %to_rows.1 = (bf16[1,256,768]{2,1,0:T(8,128)(2,1)}, bf16[1,256,768]{2,1,0:T(8,128)(2,1)}, bf16[1,256,768]{2,1,0:T(8,128)(2,1)}, f32[1,128]{1,0:T(1,128)}, f32[1,128]{1,0:T(1,128)}) custom-call(bf16[256,256]{1,0:T(8,128)(2,1)} %get-tuple-element.13.back_ref, bf16[3,1536,128]{2,1,0:T(8,128)(2,1)} %get-tuple-element.14.slots_ref, ...), custom_call_target="tpu_custom_call" | custom-call | flops 300000000 | bytes 3000000 | tf_op jit(solution)/shard_map/to_rows/pallas_call | solution.py:660

commit v11 on v10

--- a/solution.py
+++ b/solution.py
@@ -271,7 +271,7 @@
 
     route(0, 0, TARGETS)
     to_slots(1, q_ref)
-    route(1, 0, TARGETS // 2)
+    route(1, 0, TARGETS)
     to_slots(2, v_ref)
     to_slots(3, g_ref)
 
@@ -491,30 +491,28 @@
         build_pick()
         to_dense(0)
 
-    route(1, TARGETS // 2, TARGETS, beside=0)
-    route(2, 0, TARGETS)
+    route(2, 0, TARGETS, beside=0)
 
     @pl.when(active)
     def _():
+        to_dense(1)
+
+    route(3, 0, TARGETS // 2, beside=1)
+
+    @pl.when(active)
+    def _():
         terms[...] = jnp.zeros_like(terms)
-        to_dense(1)
         gather_pass(0)
         gather_finish(0)
-        lax.fori_loop(0, 1, score_tile, 0)
-
-    route(3, 0, TARGETS // 2, beside=1)
+        lax.fori_loop(0, TILES // 2, score_tile, 0)
+        to_dense(2)
+
+    route(3, TARGETS // 2, TARGETS, beside=2)
 
     @pl.when(active)
     def _():
-        lax.fori_loop(1, TILES // 2, score_tile, 0)
-        to_dense(2)
-
-    route(3, TARGETS // 2, TARGETS, beside=2)
-
-    @pl.when(active)
-    def _():
+        gather_pass(1)
         lax.fori_loop(TILES // 2, TILES, score_tile, 0)
-        gather_pass(1)
         gather_pass(2)
         to_dense(3)
         gather_rest()

time: 124 us -> 119 us (0.960)
  Pallas kernels: 123 us -> 118 us
    pallas_call x1, Pallas kernels: 121 us -> 116 us  [core(): pl.pallas_call(core_kernel, name='core', in_specs=[in_vmem] * 7, out_spec...]
where the time goes in v11:
time: 119 us
  Pallas kernels  118 us (99%)
    pallas_call x1, Pallas kernels, core(): pl.pallas_call(core_kernel, name='core', in_specs=[in_vmem] * 7, out_spec...  116 us
    pallas_call x1, Pallas kernels, to_rows(): pl.pallas_call(rows_kernel, name='to_rows', grid=(parts,), in_specs=[pl.B...  2.8 us

profile of v11, /device:TPU:1, one launch (start us, length us, event | category | flops | bytes accessed | tf_op | source)
XLA Modules:
  0.0 119.2 jit_solution(16993781529778257676)
XLA Ops:
  0.6 115.7 %core.1 = (bf16[3,1536,128]{2,1,0:T(8,128)(2,1)}, bf16[256,256]{1,0:T(8,128)(2,1)}, f32[16,128]{1,0:T(8,128)}) custom-call(s32[32,128]{1,0:T(8,128)} %bitcast.13, bf16[256,768]{1,0:T(8,128)(2,1)} %bitcast.9, bf16[256,768]{1,0:T(8,128)(2,1)} %bitcast.10, bf16[256,768]{1,0:T(8,128)(2,1)} %bitcast.11, bf16[256,768]{1,0:T(8,128)(2,1)} %bitcast.12, ...), custom_call_target="tpu_custom_call" | custom-call | tf_op jit(solution)/shard_map/core/pallas_call | solution.py:594
  116.3 2.8 %to_rows.1 = (bf16[1,256,768]{2,1,0:T(8,128)(2,1)}, bf16[1,256,768]{2,1,0:T(8,128)(2,1)}, bf16[1,256,768]{2,1,0:T(8,128)(2,1)}, f32[1,128]{1,0:T(1,128)}, f32[1,128]{1,0:T(1,128)}) custom-call(bf16[256,256]{1,0:T(8,128)(2,1)} %get-tuple-element.13.back_ref, bf16[3,1536,128]{2,1,0:T(8,128)(2,1)} %get-tuple-element.14.slots_ref, ...), custom_call_target="tpu_custom_call" | custom-call | flops 300000000 | bytes 3000000 | tf_op jit(solution)/shard_map/to_rows/pallas_call | solution.py:658

commit v12 on v11

--- a/solution.py
+++ b/solution.py
@@ -429,8 +429,10 @@
     def q_home(h, i):
         return q_slots.at[i, half_of(h), :], home_ref.at[0, home_half(h), :]
 
-    def kv_home(h, i):
-        return kv_slots.at[:, i, half_of(h), :], home_ref.at[1:3, home_half(h), :]
+    def kv_home(first, count, i):
+        rows = pl.ds(pl.multiple_of(first, PART), count)
+        home_rows = pl.ds(pl.multiple_of(seat * CHUNK + first, PART), count)
+        return kv_slots.at[:, i, rows, :], home_ref.at[1:3, home_rows, :]
 
     def send_home(copies, sem):
         def start(n, _):
@@ -472,9 +474,13 @@
         for i, result in enumerate((grads, value_grad)):
             kv_slots[i, :, part_of(t), :] = spread_tile(t, result)
 
-        @pl.when((t & 1) == 1)
-        def _():
-            send_home(lambda i: kv_home(t >> 1, i), 1)
+        @pl.when(t == 1)
+        def _():
+            send_home(lambda i: kv_home(0, 2 * PART, i), 1)
+
+        @pl.when(t > 1)
+        def _():
+            send_home(lambda i: kv_home(t * PART, PART, i), 1)
 
         return 0
 

time: 119 us -> 119 us (level)
  no operation moved by 1% of the time
where the time goes in v12:
time: 119 us
  Pallas kernels  118 us (99%)
    pallas_call x1, Pallas kernels, core(): pl.pallas_call(core_kernel, name='core', in_specs=[in_vmem] * 7, out_spec...  116 us
    pallas_call x1, Pallas kernels, to_rows(): pl.pallas_call(rows_kernel, name='to_rows', grid=(parts,), in_specs=[pl.B...  2.8 us

profile of v12, /device:TPU:1, one launch (start us, length us, event | category | flops | bytes accessed | tf_op | source)
XLA Modules:
  0.0 119.2 jit_solution(340497125374939380)
XLA Ops:
  0.6 115.7 %core.1 = (bf16[3,1536,128]{2,1,0:T(8,128)(2,1)}, bf16[256,256]{1,0:T(8,128)(2,1)}, f32[16,128]{1,0:T(8,128)}) custom-call(s32[32,128]{1,0:T(8,128)} %bitcast.13, bf16[256,768]{1,0:T(8,128)(2,1)} %bitcast.9, bf16[256,768]{1,0:T(8,128)(2,1)} %bitcast.10, bf16[256,768]{1,0:T(8,128)(2,1)} %bitcast.11, bf16[256,768]{1,0:T(8,128)(2,1)} %bitcast.12, ...), custom_call_target="tpu_custom_call" | custom-call | tf_op jit(solution)/shard_map/core/pallas_call | solution.py:600
  116.3 2.8 %to_rows.1 = (bf16[1,256,768]{2,1,0:T(8,128)(2,1)}, bf16[1,256,768]{2,1,0:T(8,128)(2,1)}, bf16[1,256,768]{2,1,0:T(8,128)(2,1)}, f32[1,128]{1,0:T(1,128)}, f32[1,128]{1,0:T(1,128)}) custom-call(bf16[256,256]{1,0:T(8,128)(2,1)} %get-tuple-element.13.back_ref, bf16[3,1536,128]{2,1,0:T(8,128)(2,1)} %get-tuple-element.14.slots_ref, ...), custom_call_target="tpu_custom_call" | custom-call | flops 300000000 | bytes 3000000 | tf_op jit(solution)/shard_map/to_rows/pallas_call | solution.py:664
